TPU v7x, 256 devices: a whole 4x4x8 slice. The times are simulated.
256 devices in a mesh: leaf: 64 (over y, z, core), slab: 4 (over x).
Axes of the slice: x: 4, y: 4, z: 8, core: 2. Of those that a mesh axis runs over, the one named last changes fastest.
Arguments:
- rhs: bfloat16 [8, 1048576], P(None, ('leaf', 'slab')), may hold values from -6 to 6
- col_basis: bfloat16 [4096, 64, 256], P(('leaf', 'slab')), may hold values from -0.375 to 0.375
- row_basis: bfloat16 [4096, 64, 256], P(('leaf', 'slab')), may hold values from -0.75 to 0.75
- near_blocks: bfloat16 [4096, 3, 256, 256], P(('leaf', 'slab')), may hold values from -0.21875 to 0.21875
- near_partner: int32 [4096, 3], P(('leaf', 'slab')), may hold values from 0 to 4095, as said below
- near_count: int32 [4096], P(('leaf', 'slab')), may hold values from 2 to 3
- col_transfer_local: float32 [7680, 64, 64], P(('leaf', 'slab')), may hold values from -0.5 to 0.5
- row_transfer_local: float32 [7680, 64, 64], P(('leaf', 'slab')), may hold values from -0.75 to 0.75
- local_coupling: float32 [7168, 4, 64, 64], P(('leaf', 'slab')), may hold values from -0.375 to 0.375
- local_partner: int32 [7168, 4], P(('leaf', 'slab')), may hold values from 0 to 4095
- local_count: int32 [7168], P(('leaf', 'slab')), may hold values from 0 to 4, as said below
- col_transfer_up: float32 [256, 6, 64, 64], P(('leaf', 'slab')), as said below
- row_transfer_up: float32 [256, 6, 64, 64], P(('leaf', 'slab')), as said below
- up_coupling: float32 [256, 7, 4, 64, 64], P(('leaf', 'slab')), as said below
- up_partner: int32 [256, 7, 4], P(('leaf', 'slab')), may hold values from 0 to 255, as said below
- up_count: int32 [256, 7], P(('leaf', 'slab')), may hold values from 0 to 4, as said below
Outputs:
- result: float32 [8, 1048576], P(None, ('leaf', 'slab'))
Inputs may be any that keep to these rules, and one draw needn't show every extreme that they name: `near_partner`: slot 0 of leaf i holds i. Slot 1 holds a leaf 1 or 2 places above i when i mod 16 >= 8, and 1 or 2 places below i otherwise. Slot 2 holds a leaf 1 or 2 places on the other side. Where a side has no such leaf (the ends of the range), leaves 1 and 2 places on the existing side are used. All three slots are distinct. `local_count`: at most the number of clusters 2 or 3 places from the cluster that exist. `up_partner`: entry [d, u] describes the ancestor j = d div 2^u of device d at level log2 16 + u and is the same for all devices with that ancestor; its first up_count slots hold distinct clusters 2 or 3 places from j, the remaining slots hold j. `up_count`: same for all devices with a common ancestor at that level; at most the number of clusters 2 or 3 places away that exist. `col_transfer_up`: entry [d, u] is the same for all devices with a common ancestor at level log2 16 + u. `row_transfer_up`: entry [d, u] is the same for all devices with a common ancestor at level log2 16 + u. `up_coupling`: entry [d, u] is the same for all devices with a common ancestor at level log2 16 + u.
All inputs are finite; a program needn't handle non-finite values.
Results may differ from a plain program's by a relative error of at most 0.0029.
Values may be sent and summed in bfloat16 or wider, within the bound.
No kernel may reach another device: no remote copies, remote signals or barrier semaphores. Data moves between devices by JAX's collectives and lax.ppermute only.
A program may use at most 64 MiB of HBM per device.

v0:
```python
import jax
import jax.numpy as jnp
from jax import lax
from jax.sharding import PartitionSpec as P


def with_halo(block, sides, width):
    for axis, dim in sides:
        count = lax.axis_size(axis)
        forward = [(i, i + 1) for i in range(count - 1)]
        backward = [(target, source) for source, target in forward]
        low = lax.ppermute(
            lax.slice_in_dim(block, block.shape[dim] - width, None, axis=dim), axis, forward
        )
        high = lax.ppermute(lax.slice_in_dim(block, 0, width, axis=dim), axis, backward)
        block = jnp.concatenate([low, block, high], axis=dim)
    return block


def precise(form, left, right):
    return jnp.einsum(form, left, right, precision=lax.Precision.HIGHEST)


def body(
    rhs,
    col_basis,
    row_basis,
    near_blocks,
    near_partner,
    near_count,
    col_transfer_local,
    row_transfer_local,
    local_coupling,
    local_partner,
    local_count,
    col_transfer_up,
    row_transfer_up,
    up_coupling,
    up_partner,
    up_count,
):
    ndev = lax.axis_size(("leaf", "slab"))
    mine = lax.axis_index(("leaf", "slab"))
    leaves, rank, leaf_len = col_basis.shape
    nrhs = rhs.shape[0]
    depth = leaves.bit_length() - 1
    slots = local_partner.shape[1]
    near_slots = near_partner.shape[1]
    starts = [sum((leaves >> g for g in range(level))) for level in range(depth)]
    points = rhs.reshape(nrhs, leaves, leaf_len)
    upward = [jnp.einsum("rlp,lkp->lrk", points, col_basis, preferred_element_type=jnp.float32)]
    for level in range(depth):
        width = leaves >> level
        moved = precise(
            "irk,ikj->irj", upward[-1], col_transfer_local[starts[level] : starts[level] + width]
        )
        upward.append(moved.reshape(width // 2, 2, nrhs, rank).sum(axis=1))
    coupled = depth - 1
    flats = [upward[level].reshape(leaves >> level, nrhs * rank) for level in range(coupled)]
    padded = [with_halo(flat, ((("leaf", "slab"), 0),), 3) for flat in flats]
    far_terms = []
    for level in range(coupled):
        width = leaves >> level
        partner = local_partner[starts[level] : starts[level] + width]
        count = local_count[starts[level] : starts[level] + width]
        spot = partner - mine * width + 3
        live = jnp.arange(slots)[None, :] < count[:, None]
        picker = (
            (spot[:, :, None] == jnp.arange(width + 6)[None, None, :]) & live[:, :, None]
        ).astype(jnp.float32)
        chosen = precise("isj,jm->ism", picker, padded[level]).reshape(width, slots, nrhs, rank)
        far_terms.append(
            precise("isrk,iskj->irj", chosen, local_coupling[starts[level] : starts[level] + width])
        )
    root = upward[depth].reshape(nrhs, rank)
    tiers = up_partner.shape[1]
    coarse_terms = []
    shares = [root]
    chain = root
    for tier in range(tiers - 1):
        chain = precise("rk,kj->rj", chain, col_transfer_up[0, tier])
        shares.append(chain)
    everyone = lax.all_gather(jnp.stack(shares)[None], ("leaf", "slab"), axis=0, tiled=True)
    for tier in range(tiers):
        span = 1 << tier
        totals = everyone[:, tier].reshape(ndev // span, span, nrhs, rank).sum(axis=1)
        live = (jnp.arange(slots) < up_count[0, tier]).astype(jnp.float32)
        lookup = totals[up_partner[0, tier]] * live[:, None, None]
        coarse_terms.append(precise("srk,skj->rj", lookup, up_coupling[0, tier]))
    field = coarse_terms[-1]
    for tier in reversed(range(tiers - 1)):
        field = coarse_terms[tier] + precise("rk,kj->rj", field, row_transfer_up[0, tier])
    level_field = field[None]
    for level in reversed(range(depth)):
        width = leaves >> level
        spread = jnp.repeat(level_field, 2, axis=0)
        moved = precise(
            "irk,ikj->irj", spread, row_transfer_local[starts[level] : starts[level] + width]
        )
        if level < coupled:
            level_field = far_terms[level] + moved
        else:
            level_field = moved
    leaf_field = level_field.astype(jnp.bfloat16)
    far_out = jnp.einsum("lrk,lkp->rlp", leaf_field, row_basis, preferred_element_type=jnp.float32)
    edged_points = with_halo(rhs, ((("leaf", "slab"), 1),), 2 * leaf_len)
    window = edged_points.reshape(nrhs, leaves + 4, leaf_len)
    spot = near_partner - mine * leaves + 2
    live = jnp.arange(near_slots)[None, :] < near_count[:, None]
    picker = (
        (spot[:, :, None] == jnp.arange(leaves + 4)[None, None, :]) & live[:, :, None]
    ).astype(jnp.bfloat16)
    taken = jnp.einsum("lsj,rjq->lsrq", picker, window, preferred_element_type=jnp.float32).astype(
        jnp.bfloat16
    )
    near = jnp.einsum("lspq,lsrq->rlp", near_blocks, taken, preferred_element_type=jnp.float32)
    return (near + far_out).reshape(nrhs, leaves * leaf_len)


def solution(mesh):
    return jax.shard_map(
        body,
        mesh=mesh,
        in_specs=(
            P(None, ("leaf", "slab")),
            P(("leaf", "slab"), None, None),
            P(("leaf", "slab"), None, None),
            P(("leaf", "slab"), None, None, None),
            P(("leaf", "slab"), None),
            P(("leaf", "slab")),
            P(("leaf", "slab"), None, None),
            P(("leaf", "slab"), None, None),
            P(("leaf", "slab"), None, None, None),
            P(("leaf", "slab"), None),
            P(("leaf", "slab")),
            P(("leaf", "slab"), None, None, None),
            P(("leaf", "slab"), None, None, None),
            P(("leaf", "slab"), None, None, None, None),
            P(("leaf", "slab"), None, None),
            P(("leaf", "slab"), None),
        ),
        out_specs=P(None, ("leaf", "slab")),
        check_vma=False,
    )
```

profile of v0, /device:TPU:1, one launch (start us, length us, event | category | flops | bytes accessed | tf_op | source)
XLA Modules:
  0.0 185.6 jit_solution(15783813727904181830)
XLA Ops:
  6.5 1.4 fusion.129
  7.9 1.6 bitcast_reduce_fusion.6
  9.5 1.3 bitcast_reduce_fusion.7
  10.8 1.1 bitcast_reduce_fusion.8
  11.9 1.1 constant_dynamic-update-slice_fusion.5
  13.0 0.9 constant_dynamic-update-slice_fusion.4
  19.1 3.9 %collective-permute-start.6 = (f32[3,512]{1,0:T(4,128)S(1)}, f32[3,512]{1,0:T(4,128)S(1)}, u32[]{:S(2)}, u32[]{:S(2)}) collective-permute-start(f32[3,512]{1,0:T(4,128)S(1)} %slice.234), channel_id=1, source_target_pairs={{0,1},{1,2},{2,3},{3,4},{4,5},{5,6},{6,7},{7,8},{8,9},{9,10},{10,1... | collective-permute-start | bytes 18440 | tf_op jit(solution)/shard_map/ppermute | solution.py:12
  23.2 3.7 %collective-permute-start.7 = (f32[3,512]{1,0:T(4,128)S(1)}, f32[3,512]{1,0:T(4,128)S(1)}, u32[]{:S(2)}, u32[]{:S(2)}) collective-permute-start(f32[3,512]{1,0:T(4,128)S(1)} %slice.236), channel_id=1, source_target_pairs={{1,0},{2,1},{3,2},{4,3},{5,4},{6,5},{7,6},{8,7},{9,8},{10,9},{11,1... | collective-permute-start | bytes 18440 | tf_op jit(solution)/shard_map/ppermute | solution.py:15
  27.0 1.9 %collective-permute-start.4 = (f32[3,512]{1,0:T(4,128)S(1)}, f32[3,512]{1,0:T(4,128)S(1)}, u32[]{:S(2)}, u32[]{:S(2)}) collective-permute-start(f32[3,512]{1,0:T(4,128)S(1)} %slice.226), channel_id=1, source_target_pairs={{0,1},{1,2},{2,3},{3,4},{4,5},{5,6},{6,7},{7,8},{8,9},{9,10},{10,1... | collective-permute-start | bytes 18440 | tf_op jit(solution)/shard_map/ppermute | solution.py:12
  29.0 4.8 %collective-permute-start.5 = (f32[3,512]{1,0:T(4,128)S(1)}, f32[3,512]{1,0:T(4,128)S(1)}, u32[]{:S(2)}, u32[]{:S(2)}) collective-permute-start(f32[3,512]{1,0:T(4,128)S(1)} %slice.228), channel_id=1, source_target_pairs={{1,0},{2,1},{3,2},{4,3},{5,4},{6,5},{7,6},{8,7},{9,8},{10,9},{11,1... | collective-permute-start | bytes 18440 | tf_op jit(solution)/shard_map/ppermute | solution.py:15
  33.9 1.9 %collective-permute-start.2 = (f32[3,512]{1,0:T(4,128)S(1)}, f32[3,512]{1,0:T(4,128)S(1)}, u32[]{:S(2)}, u32[]{:S(2)}) collective-permute-start(f32[3,512]{1,0:T(4,128)S(1)} %slice.218), channel_id=1, source_target_pairs={{0,1},{1,2},{2,3},{3,4},{4,5},{5,6},{6,7},{7,8},{8,9},{9,10},{10,1... | collective-permute-start | bytes 18440 | tf_op jit(solution)/shard_map/ppermute | solution.py:12
  38.1 1.6 fusion.128
  39.7 1.2 compare_convert_fusion.1
  40.9 1.2 compare_convert_fusion
  42.1 1.1 compare_convert_fusion.2
  43.2 1.1 compare_convert_fusion.3
  44.3 1.3 compare_convert_fusion.4
  45.5 1.2 compare_convert_fusion.5
  46.7 1.2 slice_reduce_fusion
  56.6 1.2 compare_convert_fusion.6
  58.2 4.8 %collective-permute-start.3 = (f32[3,512]{1,0:T(4,128)S(1)}, f32[3,512]{1,0:T(4,128)S(1)}, u32[]{:S(2)}, u32[]{:S(2)}) collective-permute-start(f32[3,512]{1,0:T(4,128)S(1)} %slice.220), channel_id=1, source_target_pairs={{1,0},{2,1},{3,2},{4,3},{5,4},{6,5},{7,6},{8,7},{9,8},{10,9},{11,1... | collective-permute-start | bytes 18440 | tf_op jit(solution)/shard_map/ppermute | solution.py:15
  63.1 1.9 %collective-permute-start = (bf16[8,512]{1,0:T(8,128)(2,1)S(1)}, bf16[8,512]{1,0:T(8,128)(2,1)S(1)}, u32[]{:S(2)}, u32[]{:S(2)}) collective-permute-start(bf16[8,512]{1,0:T(8,128)(2,1)S(1)} %get-tuple-element.21), channel_id=1, source_target_pairs={{0,1},{1,2},{2,3},{3,4},{4,5},{5,6},{6,7},{7,8},{8,9},{9,10},{10,1... | collective-permute-start | bytes 24584 | tf_op jit(solution)/shard_map/ppermute | solution.py:12
  65.3 4.9 %collective-permute-start.1 = (bf16[8,512]{1,0:T(8,128)(2,1)S(1)}, bf16[8,512]{1,0:T(8,128)(2,1)S(1)}, u32[]{:S(2)}, u32[]{:S(2)}) collective-permute-start(bf16[8,512]{1,0:T(8,128)(2,1)S(1)} %get-tuple-element.22), channel_id=1, source_target_pairs={{1,0},{2,1},{3,2},{4,3},{5,4},{6,5},{7,6},{8,7},{9,8},{10,9},{11,1... | collective-permute-start | bytes 24584 | tf_op jit(solution)/shard_map/ppermute | solution.py:15
  70.9 2.5 %convolution_bitcast_fusion.1 = f32[8,8,64]{2,1,0:T(8,128)} fusion(f32[8,4,8,64]{3,2,0,1:T(8,128)S(1)} %reshape.384, f32[28,4,64,64]{3,2,1,0:T(8,128)} %param.24), kind=kOutput, calls=%fused_computation.15 | convolution fusion | flops 12582912 | bytes 1130496 | tf_op jit(solution)/shard_map/isrk,iskj->irj/dot_general | solution.py:21
  73.4 2.7 %fusion.2 = f32[16,8,64]{2,1,0:T(8,128)S(1)} fusion(f32[16,4,8,64]{3,2,0,1:T(8,128)S(1)} %reshape.381, f32[28,4,64,64]{3,2,1,0:T(8,128)} %param.24), kind=kOutput, calls=%fused_computation.11 | convolution fusion | flops 25165824 | bytes 2260992 | tf_op jit(solution)/shard_map/isrk,iskj->irj/dot_general | solution.py:21
  76.1 2.0 %convolution_bitcast_fusion.2 = f32[4,8,64]{2,1,0:T(8,128)} fusion(f32[4,4,8,64]{3,2,1,0:T(8,128)S(1)} %reshape.387, f32[28,4,64,64]{3,2,1,0:T(8,128)} %param.24), kind=kOutput, calls=%fused_computation.17 | convolution fusion | flops 6291456 | bytes 565248 | tf_op jit(solution)/shard_map/isrk,iskj->irj/dot_general | solution.py:21
  78.4 5.2 %convolution_bitcast_fusion = f32[16,8,256]{2,1,0:T(8,128)} fusion(bf16[16,3,256,256]{3,2,1,0:T(8,128)(2,1)} %param.19, bf16[16,3,8,256]{3,0,2,1:T(8,128)(2,1)S(1)} %fusion.32), kind=kOutput, calls=%fused_computation.10 | convolution fusion | flops 50331648 | bytes 6619136 | tf_op jit(solution)/shard_map/lspq,lsrq->rlp/dot_general | solution.py:116
  83.5 57.0 %all-gather.3.cloned.1.call-done = f32[1792,8,64]{2,1,0:T(8,128)} async-done(((f32[7,8,64]{2,1,0:T(8,128)}), f32[1792,8,64]{2,1,0:T(8,128)}) %all-gather.3.cloned.1.call-update) | async-done | bytes 3670032 | tf_op jit(solution)/shard_map/all_gather | solution.py:83
  140.6 3.7 %fusion.123 = (f32[256,1,8,64]{3,2,1,0:T(8,128)S(1)}, f32[256,1,8,64]{3,2,1,0:T(8,128)S(1)}, f32[256,1,8,64]{3,2,1,0:T(8,128)S(1)}, f32[256,1,8,64]{3,2,1,0:T(8,...) fusion(f32[256,7,8,64]{3,2,1,0:T(8,128)} %bitcast.226), kind=kLoop, calls=%fused_computation.207 | loop fusion | bytes 7340032 | tf_op jit(solution)/shard_map/slice | solution.py:86
  147.3 0.9 bitcast_reduce_fusion.5
  148.2 2.0 %gather_fusion.5 = f32[4,8,64]{2,1,0:T(8,128)} fusion(f32[8,8,64]{2,1,0:T(8,128)} %bitcast_reduce_fusion.1, s32[1024]{0:T(1024)} %pad_clamp_fusion.1), kind=kCustom, calls=%fused_computation.5 | custom fusion | bytes 16400 | tf_op jit(solution)/shard_map/gather | solution.py:88
  150.2 1.3 gather_fusion.6
  151.5 1.6 convolution_bitcast_fusion.4
  153.1 1.6 convolution_bitcast_fusion.3
  154.7 1.5 gather_fusion.4
  156.2 1.0 convolution_bitcast_fusion.5
  158.1 1.5 convolution_add_fusion.8
  159.6 1.6 gather_fusion.3
  162.0 1.5 convolution_add_fusion.7
  163.5 1.6 gather_fusion.2
  165.2 1.0 convolution_bitcast_fusion.7
  166.1 1.5 convolution_add_fusion.6
  167.6 1.7 gather_fusion.1
  170.2 1.5 convolution_add_fusion.5
  172.4 1.0 convolution_bitcast_fusion.9
  174.4 0.9 convolution_add_fusion.3
  175.4 1.1 convolution_add_fusion.2
  177.0 1.8 convolution_add_fusion
  (85 shorter events, 25.9 us)
Async XLA Ops:
  6.5 170.5 %copy-start = (bf16[16,64,256]{2,1,0:T(8,128)(2,1)S(1)}, bf16[16,64,256]{2,1,0:T(8,128)(2,1)}, u32[]{:S(2)}) copy-start(bf16[16,64,256]{2,1,0:T(8,128)(2,1)} %param.18) | copy-start | bytes 1572868
  6.5 134.0 %all-gather.3.cloned.1.call-start = ((), (), s32[]{:S(2)}) async-start(), calls=%async_computation | async-start | bytes 7368704 | tf_op jit(solution)/shard_map/all_gather | solution.py:83
  7.9 70.2 %copy-start.3 = (bf16[8,4096]{1,0:T(8,128)(2,1)S(1)}, bf16[8,4096]{1,0:T(8,128)(2,1)}, u32[]{:S(2)}) copy-start(bf16[8,4096]{1,0:T(8,128)(2,1)} %param.16) | copy-start | bytes 196612
  18.4 0.6 copy-start.4
  19.1 46.1 %collective-permute-start.6 = (f32[3,512]{1,0:T(4,128)S(1)}, f32[3,512]{1,0:T(4,128)S(1)}, u32[]{:S(2)}, u32[]{:S(2)}) collective-permute-start(f32[3,512]{1,0:T(4,128)S(1)} %slice.234), channel_id=1, source_target_pairs={{0,1},{1,2},{2,3},{3,4},{4,5},{5,6},{6,7},{7,8},{8,9},{9,10},{10,1... | collective-permute-start | bytes 18440 | tf_op jit(solution)/shard_map/ppermute | solution.py:12
  23.2 47.0 %collective-permute-start.7 = (f32[3,512]{1,0:T(4,128)S(1)}, f32[3,512]{1,0:T(4,128)S(1)}, u32[]{:S(2)}, u32[]{:S(2)}) collective-permute-start(f32[3,512]{1,0:T(4,128)S(1)} %slice.236), channel_id=1, source_target_pairs={{1,0},{2,1},{3,2},{4,3},{5,4},{6,5},{7,6},{8,7},{9,8},{10,9},{11,1... | collective-permute-start | bytes 18440 | tf_op jit(solution)/shard_map/ppermute | solution.py:15
  27.0 31.2 %collective-permute-start.4 = (f32[3,512]{1,0:T(4,128)S(1)}, f32[3,512]{1,0:T(4,128)S(1)}, u32[]{:S(2)}, u32[]{:S(2)}) collective-permute-start(f32[3,512]{1,0:T(4,128)S(1)} %slice.226), channel_id=1, source_target_pairs={{0,1},{1,2},{2,3},{3,4},{4,5},{5,6},{6,7},{7,8},{8,9},{9,10},{10,1... | collective-permute-start | bytes 18440 | tf_op jit(solution)/shard_map/ppermute | solution.py:12
  29.0 34.1 %collective-permute-start.5 = (f32[3,512]{1,0:T(4,128)S(1)}, f32[3,512]{1,0:T(4,128)S(1)}, u32[]{:S(2)}, u32[]{:S(2)}) collective-permute-start(f32[3,512]{1,0:T(4,128)S(1)} %slice.228), channel_id=1, source_target_pairs={{1,0},{2,1},{3,2},{4,3},{5,4},{6,5},{7,6},{8,7},{9,8},{10,9},{11,1... | collective-permute-start | bytes 18440 | tf_op jit(solution)/shard_map/ppermute | solution.py:15
  33.9 36.6 %collective-permute-start.2 = (f32[3,512]{1,0:T(4,128)S(1)}, f32[3,512]{1,0:T(4,128)S(1)}, u32[]{:S(2)}, u32[]{:S(2)}) collective-permute-start(f32[3,512]{1,0:T(4,128)S(1)} %slice.218), channel_id=1, source_target_pairs={{0,1},{1,2},{2,3},{3,4},{4,5},{5,6},{6,7},{7,8},{8,9},{9,10},{10,1... | collective-permute-start | bytes 18440 | tf_op jit(solution)/shard_map/ppermute | solution.py:12
  58.2 12.3 %collective-permute-start.3 = (f32[3,512]{1,0:T(4,128)S(1)}, f32[3,512]{1,0:T(4,128)S(1)}, u32[]{:S(2)}, u32[]{:S(2)}) collective-permute-start(f32[3,512]{1,0:T(4,128)S(1)} %slice.220), channel_id=1, source_target_pairs={{1,0},{2,1},{3,2},{4,3},{5,4},{6,5},{7,6},{8,7},{9,8},{10,9},{11,1... | collective-permute-start | bytes 18440 | tf_op jit(solution)/shard_map/ppermute | solution.py:15
  63.1 15.0 %collective-permute-start = (bf16[8,512]{1,0:T(8,128)(2,1)S(1)}, bf16[8,512]{1,0:T(8,128)(2,1)S(1)}, u32[]{:S(2)}, u32[]{:S(2)}) collective-permute-start(bf16[8,512]{1,0:T(8,128)(2,1)S(1)} %get-tuple-element.21), channel_id=1, source_target_pairs={{0,1},{1,2},{2,3},{3,4},{4,5},{5,6},{6,7},{7,8},{8,9},{9,10},{10,1... | collective-permute-start | bytes 24584 | tf_op jit(solution)/shard_map/ppermute | solution.py:12
  65.3 12.9 %collective-permute-start.1 = (bf16[8,512]{1,0:T(8,128)(2,1)S(1)}, bf16[8,512]{1,0:T(8,128)(2,1)S(1)}, u32[]{:S(2)}, u32[]{:S(2)}) collective-permute-start(bf16[8,512]{1,0:T(8,128)(2,1)S(1)} %get-tuple-element.22), channel_id=1, source_target_pairs={{1,0},{2,1},{3,2},{4,3},{5,4},{6,5},{7,6},{8,7},{9,8},{10,9},{11,1... | collective-permute-start | bytes 24584 | tf_op jit(solution)/shard_map/ppermute | solution.py:15
  144.3 7.2 %copy-start.2 = (f32[1,7,4,64,64]{4,3,2,1,0:T(8,128)S(1)}, f32[1,7,4,64,64]{4,3,2,1,0:T(8,128)}, u32[]{:S(2)}) copy-start(f32[1,7,4,64,64]{4,3,2,1,0:T(8,128)} %param.29) | copy-start | bytes 1376260
  145.0 29.3 %copy-start.1 = (f32[30,64,64]{2,1,0:T(8,128)S(1)}, f32[30,64,64]{2,1,0:T(8,128)}, u32[]{:S(2)}) copy-start(f32[30,64,64]{2,1,0:T(8,128)} %param.23) | copy-start | bytes 1474564
Sparse Core Ops, SparseCore 0:
  19.2 121.3 all-gather.2
where the time goes:
time: 188 us; the launch traced here: 186 us
  waiting for transfers between devices  57.1 us (30%)
  matrix products  45.2 us (24%)
  starting transfers between devices  28 us (15%)
  local copies, waits for them, and re-layouts  20.8 us (11%)
  other arithmetic  20.8 us (11%)
  between operations  13.7 us (7%)
    all_gather x1, waiting for transfers between devices, body(): lax.all_gather(jnp.stack(shares)[None], ('leaf', 'slab'), axis=0, tiled=T...  57 us
    dot_general x33, matrix products, precise(): return jnp.einsum(form, left, right, precision=lax.Precision.HIGHEST)  36.7 us
    ppermute x4, starting transfers between devices, with_halo(): lax.ppermute(lax.slice_in_dim(block, 0, width, axis=dim), axis, backward)  18.3 us
    gather x7, local copies, waits for them, and re-layouts, body(): lookup = totals[up_partner[0, tier]] * live[:, None, None]  10.4 us
    ppermute x4, starting transfers between devices, with_halo(): lax.ppermute(lax.slice_in_dim(block, block.shape[dim] - width, None, axis...  9.68 us
    convert_element_type x7, other arithmetic, body(): live = (jnp.arange(slots) < up_count[0, tier]).astype(jnp.float32)  8.27 us
    dot_general x1, matrix products, body(): jnp.einsum('lspq,lsrq->rlp', near_blocks, taken, preferred_element_type=j...  5.17 us
    gather x7, other arithmetic, body(): lookup = totals[up_partner[0, tier]] * live[:, None, None]  4.15 us
  transfers between devices with their start and end apart: 9, of which 1 were waited for; matrix products, arithmetic and copies ran while one was open for 20% of the time, Pallas kernels for 0%

commit v1 on v0

v1 whole, which is shorter than its diff:
```python
import jax
import jax.numpy as jnp
from jax import lax
from jax.experimental import pallas as pl
from jax.experimental.pallas import tpu as pltpu
from jax.sharding import PartitionSpec as P

AXES = ("leaf", "slab")
F32 = jnp.float32
BF16 = jnp.bfloat16
LEAVES = 16
LEAF_LEN = 256
RANK = 64
NRHS = 8
TIERS = 7
SLOTS = 4
NDEV = 256
STARTS = (0, 16, 24, 28)
ROWS = (0, 16, 24)
EDGE = 2 * LEAF_LEN
HALO = EDGE + 10 * RANK
ZERO = 6


def mxu(left, right):
    return lax.dot_general(left, right, (((1,), (0,)), ((), ())), preferred_element_type=F32)


def mxu_t(left, right):
    return lax.dot_general(left, right, (((1,), (1,)), ((), ())), preferred_element_type=F32)


def split(value):
    high = value.astype(BF16)
    return high, (value - high.astype(F32)).astype(BF16)


def stacked(value):
    high = value.astype(BF16).astype(F32)
    return jnp.concatenate([high, value - high], axis=0).astype(BF16)


def folded(left, high, low):
    total = mxu(left, high) + mxu(left, low)
    half = total.shape[0] // 2
    return total[:half] + total[half:]


def product(left, right):
    return folded(stacked(left), *split(right))


def up_kernel(rhs, col_basis, col_local, col_up, blocks, coeffs, halo_up, halo_down):
    me = lax.axis_index("leaf") * 4 + lax.axis_index("slab")
    blocks[...] = jnp.zeros_like(blocks)
    level = [
        mxu_t(rhs[:, l * LEAF_LEN : (l + 1) * LEAF_LEN], col_basis[l]) for l in range(LEAVES)
    ]
    spot = 0
    for h in range(4):
        width = LEAVES >> h
        if h < 3:
            for c in range(width):
                coeffs[ROWS[h] + c] = level[c]
            for i in range(3):
                at = EDGE + (h * 3 + i) * RANK
                halo_up[:, at : at + RANK] = level[width - 3 + i].astype(BF16)
                halo_down[:, at : at + RANK] = level[i].astype(BF16)
        above = []
        for j in range(width // 2):
            pair = jnp.concatenate([level[2 * j], level[2 * j + 1]], axis=1)
            moves = col_local[STARTS[h] + 2 * j : STARTS[h] + 2 * j + 2].reshape(2 * RANK, RANK)
            above.append(product(pair, moves))
        level = above
    halo_up[:, :EDGE] = rhs[:, (LEAVES - 2) * LEAF_LEN :]
    halo_down[:, :EDGE] = rhs[:, :EDGE]
    halo_up[:, HALO - RANK :] = jnp.zeros((NRHS, RANK), BF16)
    halo_down[:, HALO - RANK :] = jnp.zeros((NRHS, RANK), BF16)
    share = level[0]
    for u in range(TIERS):
        sent = share.astype(BF16)
        side = (u % 2) * RANK
        span = 1 << u
        own = lax.shift_right_logical(me, u)
        for off in (-3, -2, 2, 3):
            there = own + off

            @pl.when((there >= 0) & (there < (NDEV >> u)))
            def _():
                blocks[pl.ds(there * span, span), :, side : side + RANK] = jnp.broadcast_to(
                    sent[None], (span, NRHS, RANK)
                )

        if u < TIERS - 1:
            share = product(share, col_up[0, u])


def near_leaf(l, me, window, shift, blocks, partner, count):
    total = None
    for s in range(3):
        spot = partner[l, s] - me * LEAVES + shift
        part = window[:, pl.ds(pl.multiple_of(spot * LEAF_LEN, LEAF_LEN), LEAF_LEN)]
        if s == 2:
            part = jnp.where(count[l] > s, part, jnp.zeros_like(part))
        term = mxu_t(part, blocks[s])
        total = term if total is None else total + term
    return total


def inner_kernel(
    rhs, near_blocks, partner, count, row_local, row_up, coupling, near, paths, pairs, held, sems
):
    me = lax.axis_index("leaf") * 4 + lax.axis_index("slab")
    inner = LEAVES - 4
    copies = [
        pltpu.make_async_copy(near_blocks.at[2 + l], held.at[l], sems.at[l]) for l in range(inner)
    ]
    for copy in copies:
        copy.start()
    level = [row_local[STARTS[3] + c] for c in range(2)]
    for h in (2, 1, 0):
        level = [
            product(level[c // 2], row_local[STARTS[h] + c]) for c in range(LEAVES >> h)
        ]
    for l in range(LEAVES):
        high, low = split(level[l])
        paths[0, :, l * RANK : (l + 1) * RANK] = high
        paths[1, :, l * RANK : (l + 1) * RANK] = low
    for u in range(TIERS):
        high, low = split(coupling[0, u].reshape(SLOTS * RANK, RANK))
        pairs[0, u * 256 : (u + 1) * 256] = high
        pairs[1, u * 256 : (u + 1) * 256] = low
    for u in range(TIERS - 1):
        high, low = split(row_up[0, u])
        at = TIERS * 256 + u * RANK
        pairs[0, at : at + RANK] = high
        pairs[1, at : at + RANK] = low
    for l in range(inner):
        copies[l].wait()
        near[:, l * LEAF_LEN : (l + 1) * LEAF_LEN] = near_leaf(
            l + 2, me, rhs, 0, held.at[l], partner, count
        )


def edge_kernel(
    rhs,
    from_low,
    from_high,
    coeffs,
    near_blocks,
    partner,
    count,
    coupling,
    local_partner,
    local_count,
    row_local,
    near,
    field,
    held,
    sems,
    window,
    left,
    right,
):
    me = lax.axis_index("leaf") * 4 + lax.axis_index("slab")
    leaves = (0, 1, LEAVES - 2, LEAVES - 1)
    copies = [
        pltpu.make_async_copy(near_blocks.at[l], held.at[i], sems.at[i])
        for i, l in enumerate(leaves)
    ]
    for copy in copies:
        copy.start()
    window[:, :EDGE] = from_low[:, :EDGE]
    window[:, EDGE : EDGE + LEAVES * LEAF_LEN] = rhs[...]
    window[:, EDGE + LEAVES * LEAF_LEN :] = from_high[:, :EDGE]
    blank = jnp.zeros((2 * NRHS, RANK), F32)

    def place(at, value):
        high = value.astype(BF16).astype(F32)
        both = jnp.concatenate([high, value - high], axis=0)
        left[at] = jnp.concatenate([both, blank], axis=1)
        right[at] = jnp.concatenate([blank, both], axis=1)

    far = []
    base = 0
    for h in range(3):
        width = LEAVES >> h
        for i in range(3):
            at = EDGE + (h * 3 + i) * RANK
            place(base + i, from_low[:, at : at + RANK].astype(F32))
            place(base + 3 + width + i, from_high[:, at : at + RANK].astype(F32))
        for c in range(width):
            place(base + 3 + c, coeffs[ROWS[h] + c])
        none = base + width + ZERO
        left[none] = jnp.zeros((2 * NRHS, 2 * RANK), F32)
        right[none] = jnp.zeros((2 * NRHS, 2 * RANK), F32)
        terms = []
        for c in range(width):
            row = ROWS[h] + c
            live = local_count[row]
            spots = [
                jnp.where(s < live, local_partner[row, s] - me * width + (base + 3), none)
                for s in range(SLOTS)
            ]
            chosen = jnp.concatenate(
                [left[spots[0]] + right[spots[1]], left[spots[2]] + right[spots[3]]], axis=1
            ).astype(BF16)
            terms.append(folded(chosen, *split(coupling[row].reshape(SLOTS * RANK, RANK))))
        far.append(terms)
        base += width + ZERO + 1
    level = far[2]
    for h in (1, 0):
        level = [
            far[h][c] + product(level[c // 2], row_local[STARTS[h] + c])
            for c in range(LEAVES >> h)
        ]
    for l in range(LEAVES):
        field[:, l * RANK : (l + 1) * RANK] = level[l]
    for i, l in enumerate(leaves):
        copies[i].wait()
        near[:, i * LEAF_LEN : (i + 1) * LEAF_LEN] = near_leaf(
            l, me, window, 2, held.at[i], partner, count
        )


def final_kernel(
    got, partner, count, pairs, paths, field, near_inner, near_edge, row_basis, out
):
    lane = lax.broadcasted_iota(jnp.int32, (NRHS, 2 * RANK), 1)
    far = []
    for u in range(TIERS):
        span = 1 << u
        live = count[0, u]
        sums = []
        for s in range(SLOTS):
            block = got[pl.ds(partner[0, u, s] * span, span)].astype(F32)
            total = jnp.where(s < live, jnp.sum(block, axis=0), 0.0)
            sums.append(total if s % 2 == u % 2 else pltpu.roll(total, RANK, 1))
        chosen = jnp.concatenate(
            [
                jnp.where(lane < RANK, sums[0], sums[1]),
                jnp.where(lane < RANK, sums[2], sums[3]),
            ],
            axis=1,
        )
        rows = slice(u * 256, (u + 1) * 256)
        far.append(folded(stacked(chosen), pairs[0, rows], pairs[1, rows]))
    down = far[TIERS - 1]
    for u in reversed(range(TIERS - 1)):
        at = TIERS * 256 + u * RANK
        rows = slice(at, at + RANK)
        down = far[u] + folded(stacked(down), pairs[0, rows], pairs[1, rows])
    leaf_field = field[...] + folded(stacked(down), paths[0], paths[1])
    both = stacked(leaf_field)
    for l in range(LEAVES):
        total = mxu(both[:, l * RANK : (l + 1) * RANK], row_basis[l])
        if 2 <= l < LEAVES - 2:
            near = near_inner[:, (l - 2) * LEAF_LEN : (l - 1) * LEAF_LEN]
        else:
            i = l if l < 2 else l - (LEAVES - 4)
            near = near_edge[:, i * LEAF_LEN : (i + 1) * LEAF_LEN]
        out[:, l * LEAF_LEN : (l + 1) * LEAF_LEN] = near + total[:NRHS] + total[NRHS:]


VMEM = pl.BlockSpec(memory_space=pltpu.VMEM)
SMEM = pl.BlockSpec(memory_space=pltpu.SMEM)
ANY = pl.BlockSpec(memory_space=pl.ANY)
LIMIT = pltpu.CompilerParams(vmem_limit_bytes=24 * 1024 * 1024)


def cost(flops, size):
    return pl.CostEstimate(flops=flops, bytes_accessed=size, transcendentals=0)


def body(
    rhs,
    col_basis,
    row_basis,
    near_blocks,
    near_partner,
    near_count,
    col_transfer_local,
    row_transfer_local,
    local_coupling,
    local_partner,
    local_count,
    col_transfer_up,
    row_transfer_up,
    up_coupling,
    up_partner,
    up_count,
):
    shape = jax.ShapeDtypeStruct
    blocks, coeffs, halo_up, halo_down = pl.pallas_call(
        up_kernel,
        out_shape=(
            shape((NDEV, NRHS, 2 * RANK), BF16),
            shape((28, NRHS, RANK), F32),
            shape((NRHS, HALO), BF16),
            shape((NRHS, HALO), BF16),
        ),
        in_specs=[VMEM] * 4,
        out_specs=(VMEM,) * 4,
        compiler_params=LIMIT,
        cost_estimate=cost(2 * 10**7, 4 * 10**6),
    )(rhs, col_basis, col_transfer_local, col_transfer_up)
    ups = [(i, i + 1) for i in range(NDEV - 1)]
    downs = [(i + 1, i) for i in range(NDEV - 1)]
    got = lax.all_to_all(blocks, AXES, 0, 0)
    from_low = lax.ppermute(halo_up, AXES, ups)
    from_high = lax.ppermute(halo_down, AXES, downs)
    inner = LEAVES - 4
    near_inner, paths, pairs = pl.pallas_call(
        inner_kernel,
        out_shape=(
            shape((NRHS, inner * LEAF_LEN), F32),
            shape((2, RANK, LEAVES * RANK), BF16),
            shape((2, TIERS * 256 + (TIERS - 1) * RANK, RANK), BF16),
        ),
        in_specs=[VMEM, ANY, SMEM, SMEM, VMEM, VMEM, VMEM],
        out_specs=(VMEM,) * 3,
        scratch_shapes=[
            pltpu.VMEM((inner, 3, LEAF_LEN, LEAF_LEN), BF16),
            pltpu.SemaphoreType.DMA((inner,)),
        ],
        compiler_params=LIMIT,
        cost_estimate=cost(2 * 10**8, 10**7),
    )(
        rhs,
        near_blocks,
        near_partner,
        near_count,
        row_transfer_local,
        row_transfer_up,
        up_coupling,
    )
    entries = 28 + 3 * (ZERO + 1)
    near_edge, field = pl.pallas_call(
        edge_kernel,
        out_shape=(shape((NRHS, 4 * LEAF_LEN), F32), shape((NRHS, LEAVES * RANK), F32)),
        in_specs=[VMEM, VMEM, VMEM, VMEM, ANY, SMEM, SMEM, VMEM, SMEM, SMEM, VMEM],
        out_specs=(VMEM,) * 2,
        scratch_shapes=[
            pltpu.VMEM((4, 3, LEAF_LEN, LEAF_LEN), BF16),
            pltpu.SemaphoreType.DMA((4,)),
            pltpu.VMEM((NRHS, LEAVES * LEAF_LEN + 2 * EDGE), BF16),
            pltpu.VMEM((entries, 2 * NRHS, 2 * RANK), F32),
            pltpu.VMEM((entries, 2 * NRHS, 2 * RANK), F32),
        ],
        compiler_params=LIMIT,
        cost_estimate=cost(10**8, 7 * 10**6),
    )(
        rhs,
        from_low,
        from_high,
        coeffs,
        near_blocks,
        near_partner,
        near_count,
        local_coupling,
        local_partner,
        local_count,
        row_transfer_local,
    )
    return pl.pallas_call(
        final_kernel,
        out_shape=shape((NRHS, LEAVES * LEAF_LEN), F32),
        in_specs=[VMEM, SMEM, SMEM] + [VMEM] * 6,
        out_specs=VMEM,
        compiler_params=LIMIT,
        cost_estimate=cost(2 * 10**7, 3 * 10**6),
    )(got, up_partner, up_count, pairs, paths, field, near_inner, near_edge, row_basis)


def solution(mesh):
    return jax.shard_map(
        body,
        mesh=mesh,
        in_specs=(
            P(None, AXES),
            P(AXES, None, None),
            P(AXES, None, None),
            P(AXES, None, None, None),
            P(AXES, None),
            P(AXES),
            P(AXES, None, None),
            P(AXES, None, None),
            P(AXES, None, None, None),
            P(AXES, None),
            P(AXES),
            P(AXES, None, None, None),
            P(AXES, None, None, None),
            P(AXES, None, None, None, None),
            P(AXES, None, None),
            P(AXES, None),
        ),
        out_specs=P(None, AXES),
        check_vma=False,
    )
```

time: 188 us -> 60 us (0.32)
  the two profiles are of different devices: /device:TPU:1 before, /device:TPU:24 now
where the time goes in v1:
time: 60 us; the launch traced here: 59.3 us
  starting transfers between devices  25 us (42%)
  Pallas kernels  18.3 us (30%)
  local copies, waits for them, and re-layouts  15.9 us (26%)
    unnamed x35, local copies, waits for them, and re-layouts  15.9 us
    all_to_all x1, starting transfers between devices, body(): got = lax.all_to_all(blocks, AXES, 0, 0)  14.5 us
    pallas_call x1, Pallas kernels, body(): pl.pallas_call(inner_kernel, out_shape=(shape((NRHS, inner * LEAF_LEN), F...  7.8 us
    ppermute x1, starting transfers between devices, body(): from_high = lax.ppermute(halo_down, AXES, downs)  7.14 us
    pallas_call x1, Pallas kernels, body(): pl.pallas_call(edge_kernel, out_shape=(shape((NRHS, 4 * LEAF_LEN), F32),...  4.19 us
    pallas_call x1, Pallas kernels, body(): pl.pallas_call(up_kernel, out_shape=(shape((NDEV, NRHS, 2 * RANK), BF16),...  3.47 us
    ppermute x1, starting transfers between devices, body(): from_low = lax.ppermute(halo_up, AXES, ups)  3.39 us
    pallas_call x1, Pallas kernels, body(): pl.pallas_call(final_kernel, out_shape=shape((NRHS, LEAVES * LEAF_LEN), F...  2.79 us
  transfers between devices with their start and end apart: 3, of which 0 were waited for; matrix products, arithmetic and copies ran while one was open for 4% of the time, Pallas kernels for 20%

profile of v1, /device:TPU:24, one launch (start us, length us, event | category | flops | bytes accessed | tf_op | source)
XLA Modules:
  0.0 59.3 jit_solution(2111929797401309657)
XLA Ops:
  0.0 0.0 copy-start.5
  0.0 1.2 %copy-done.5 = f32[30,64,64]{2,1,0:T(8,128)S(1)} copy-done((f32[30,64,64]{2,1,0:T(8,128)S(1)}, f32[30,64,64]{2,1,0:T(8,128)}, u32[]{:S(2)}) %copy-start.5) | copy-done | bytes 491544
  1.2 0.0 copy-start.7
  1.2 0.8 %copy-done.7 = bf16[8,4096]{1,0:T(8,128)(2,1)S(1)} copy-done((bf16[8,4096]{1,0:T(8,128)(2,1)S(1)}, bf16[8,4096]{1,0:T(8,128)(2,1)}, u32[]{:S(2)}) %copy-start.7) | copy-done | bytes 65560
  2.0 0.0 copy-start.9
  2.0 1.0 %copy-done.9 = bf16[16,64,256]{2,1,0:T(8,128)(2,1)S(1)} copy-done((bf16[16,64,256]{2,1,0:T(8,128)(2,1)S(1)}, bf16[16,64,256]{2,1,0:T(8,128)(2,1)}, u32[]{:S(2)}) %copy-start.9) | copy-done | bytes 524312
  3.1 0.0 copy-start.11
  3.1 0.9 %copy-done.11 = f32[1,6,64,64]{3,2,1,0:T(8,128)S(1)} copy-done((f32[1,6,64,64]{3,2,1,0:T(8,128)S(1)}, f32[1,6,64,64]{3,2,1,0:T(8,128)}, u32[]{:S(2)}) %copy-start.11) | copy-done | bytes 98328
  4.0 3.5 %shard_map.154 = (bf16[256,8,128]{2,1,0:T(8,128)(2,1)}, f32[28,8,64]{2,1,0:T(8,128)S(1)}, bf16[8,1152]{1,0:T(8,128)(2,1)S(1)}, bf16[8,1152]{1,0:T(8,128)(2,1)S(1)}) custom-call(bf16[8,4096]{1,0:T(8,128)(2,1)S(1)} %copy-done.7, bf16[16,64,256]{2,1,0:T(8,128)(2,1)S(1)} %copy-done.9, f32[30,64,64]{2,1,0:T(8,128)S(1)} %copy-done.5, f32[1,6,64,64]{3,2,1,0:T(8,128)S(1)} %copy-done.11), custom_call_target="tpu_custom_call" | custom-call | flops 20000000 | bytes 4000000 | tf_op jit(solution)/shard_map/pallas_call | solution.py:294
  7.5 14.5 %all-to-all-start = ((bf16[256,8,128]{2,1,0:T(8,128)(2,1)}), bf16[256,8,128]{2,1,0:T(8,128)(2,1)S(1)}, u32[]{:S(2)}, u32[]{:S(2)}) async-start(bf16[256,8,128]{2,1,0:T(8,128)(2,1)} %get-tuple-element.14), calls=%async_computation | async-start | bytes 1048576 | tf_op jit(solution)/shard_map/all_to_all | solution.py:309
  22.0 3.4 %collective-permute-start = (bf16[8,1152]{1,0:T(8,128)(2,1)S(1)}, bf16[8,1152]{1,0:T(8,128)(2,1)S(1)}, u32[]{:S(2)}, u32[]{:S(2)}) collective-permute-start(bf16[8,1152]{1,0:T(8,128)(2,1)S(1)} %get-tuple-element.17), channel_id=1, source_target_pairs={{0,1},{1,2},{2,3},{3,4},{4,5},{5,6},{6,7},{7,8},{8,9},{9,10},{10,1... | collective-permute-start | bytes 55304 | tf_op jit(solution)/shard_map/ppermute | solution.py:310
  25.4 7.1 %collective-permute-start.1 = (bf16[8,1152]{1,0:T(8,128)(2,1)S(1)}, bf16[8,1152]{1,0:T(8,128)(2,1)S(1)}, u32[]{:S(2)}, u32[]{:S(2)}) collective-permute-start(bf16[8,1152]{1,0:T(8,128)(2,1)S(1)} %get-tuple-element.18), channel_id=1, source_target_pairs={{1,0},{2,1},{3,2},{4,3},{5,4},{6,5},{7,6},{8,7},{9,8},{10,9},{11,1... | collective-permute-start | bytes 55304 | tf_op jit(solution)/shard_map/ppermute | solution.py:311
  32.5 0.8 %copy.20.partner = s32[1,7,4]{2,1,0:T(8,128)S(1)} copy(s32[1,7,4]{1,2,0:T(4,128)} %param.30) | data formatting | bytes 224 | tf_op args[14]
  33.3 0.8 %copy.17.partner = s32[16,3]{1,0:T(8,128)S(1)} copy(s32[16,3]{0,1:T(4,128)} %param.20) | data formatting | bytes 384 | tf_op args[4]
  34.0 0.8 %copy.19.local_partner = s32[28,4]{1,0:T(8,128)S(1)} copy(s32[28,4]{0,1:T(4,128)} %param.25) | data formatting | bytes 896 | tf_op args[9]
  34.8 0.0 copy-start
  34.8 2.8 %copy-done = bf16[16,3,256,256]{3,2,1,0:T(8,128)(2,1)S(1)} copy-done((bf16[16,3,256,256]{3,2,1,0:T(8,128)(2,1)S(1)}, bf16[16,3,256,256]{3,2,1,0:T(8,128)(2,1)}, u32[]{:S(2)}) %copy-start) | copy-done | bytes 6291480
  37.6 0.0 copy-start.2
  37.6 1.2 %copy-done.2 = f32[30,64,64]{2,1,0:T(8,128)S(1)} copy-done((f32[30,64,64]{2,1,0:T(8,128)S(1)}, f32[30,64,64]{2,1,0:T(8,128)}, u32[]{:S(2)}) %copy-start.2) | copy-done | bytes 491544
  38.8 0.0 copy-start.6
  38.8 1.2 %copy-done.6 = f32[1,7,4,64,64]{4,3,2,1,0:T(8,128)S(1)} copy-done((f32[1,7,4,64,64]{4,3,2,1,0:T(8,128)S(1)}, f32[1,7,4,64,64]{4,3,2,1,0:T(8,128)}, u32[]{:S(2)}) %copy-start.6) | copy-done | bytes 458776
  40.0 0.0 copy-start.8
  40.0 0.8 %copy-done.8 = bf16[8,4096]{1,0:T(8,128)(2,1)S(1)} copy-done((bf16[8,4096]{1,0:T(8,128)(2,1)S(1)}, bf16[8,4096]{1,0:T(8,128)(2,1)}, u32[]{:S(2)}) %copy-start.8) | copy-done | bytes 65560
  40.8 0.0 copy-start.12
  40.8 0.9 %copy-done.12 = f32[1,6,64,64]{3,2,1,0:T(8,128)S(1)} copy-done((f32[1,6,64,64]{3,2,1,0:T(8,128)S(1)}, f32[1,6,64,64]{3,2,1,0:T(8,128)}, u32[]{:S(2)}) %copy-start.12) | copy-done | bytes 98328
  41.8 0.0 copy-start.13
  41.8 0.7 %copy-done.13 = s32[16]{0:T(128)S(1)} copy-done((s32[16]{0:T(128)S(1)}, s32[16]{0:T(128)}, u32[]{:S(2)}) %copy-start.13) | copy-done | bytes 88
  42.4 0.0 copy-start.1
  42.4 0.0 copy-start.3
  42.4 0.0 copy-start.14
  42.4 7.8 %shard_map.155 = (f32[8,3072]{1,0:T(8,128)S(1)}, bf16[2,64,1024]{2,1,0:T(8,128)(2,1)S(1)}, bf16[2,2176,64]{2,1,0:T(8,128)(2,1)S(1)}) custom-call(bf16[8,4096]{1,0:T(8,128)(2,1)S(1)} %copy-done.8, bf16[16,3,256,256]{3,2,1,0:T(8,128)(2,1)S(1)} %copy-done, s32[16,3]{1,0:T(8,128)S(1)} %copy.17.partner, s32[16]{0:T(128)S(1)} %copy-done.13, ...), custom_call_target="tpu_custom_call" | custom-call | flops 200000000 | bytes 10000000 | tf_op jit(solution)/shard_map/pallas_call | solution.py:313
  50.2 0.0 collective-permute-done.from_low
  50.2 0.0 collective-permute-done.1.from_high
  50.2 0.0 copy-done.1
  50.3 0.0 copy-done.3
  50.3 0.0 copy-done.14
  50.3 0.0 copy-start.4
  50.3 2.0 %copy-done.4 = f32[28,4,64,64]{3,2,1,0:T(8,128)S(1)} copy-done((f32[28,4,64,64]{3,2,1,0:T(8,128)S(1)}, f32[28,4,64,64]{3,2,1,0:T(8,128)}, u32[]{:S(2)}) %copy-start.4) | copy-done | bytes 1835032
  52.3 0.0 copy-start.10
  52.3 0.0 copy-start.15
  52.3 4.2 %shard_map.156 = (f32[8,1024]{1,0:T(8,128)S(1)}, f32[8,1024]{1,0:T(8,128)S(1)}) custom-call(bf16[8,4096]{1,0:T(8,128)(2,1)S(1)} %copy-done.8, bf16[8,1152]{1,0:T(8,128)(2,1)S(1)} %collective-permute-done.from_low, bf16[8,1152]{1,0:T(8,128)(2,1)S(1)} %collective-permute-done.1.from_high, f32[28,8,64]{2,1,0:T(8,128)S(1)} %get-tuple-element.19.coeffs, ...), custom_call_target="tpu_custom_call" | custom-call | flops 100000000 | bytes 7000000 | tf_op jit(solution)/shard_map/pallas_call | solution.py:338
  56.5 0.0 all-to-all-done.got
  56.5 0.0 copy-done.10
  56.5 0.0 copy-done.15
  56.6 2.8 %shard_map.157 = f32[8,4096]{1,0:T(8,128)} custom-call(bf16[256,8,128]{2,1,0:T(8,128)(2,1)S(1)} %all-to-all-done.got, s32[1,7,4]{2,1,0:T(8,128)S(1)} %copy.20.partner, s32[1,7]{1,0:T(1,128)S(1)} %copy-done.15, bf16[2,2176,64]{2,1,0:T(8,128)(2,1)S(1)} %get-tuple-element.15.pairs, bf16[2,64,1024]{2,1,0:T(8,128)(2,1)S(1)} %get-tuple-element.16.paths, ...), custom_call_target="tpu_custom_call" | custom-call | flops 20000000 | bytes 3000000 | tf_op jit(solution)/shard_map/pallas_call | solution.py:365
Async XLA Ops:
  0.0 1.2 %copy-start.5 = (f32[30,64,64]{2,1,0:T(8,128)S(1)}, f32[30,64,64]{2,1,0:T(8,128)}, u32[]{:S(2)}) copy-start(f32[30,64,64]{2,1,0:T(8,128)} %col_local.1) | copy-start | bytes 1474564
  1.2 0.8 %copy-start.7 = (bf16[8,4096]{1,0:T(8,128)(2,1)S(1)}, bf16[8,4096]{1,0:T(8,128)(2,1)}, u32[]{:S(2)}) copy-start(bf16[8,4096]{1,0:T(8,128)(2,1)} %rhs.5) | copy-start | bytes 196612
  2.0 1.0 %copy-start.9 = (bf16[16,64,256]{2,1,0:T(8,128)(2,1)S(1)}, bf16[16,64,256]{2,1,0:T(8,128)(2,1)}, u32[]{:S(2)}) copy-start(bf16[16,64,256]{2,1,0:T(8,128)(2,1)} %col_basis.1) | copy-start | bytes 1572868
  3.1 0.9 %copy-start.11 = (f32[1,6,64,64]{3,2,1,0:T(8,128)S(1)}, f32[1,6,64,64]{3,2,1,0:T(8,128)}, u32[]{:S(2)}) copy-start(f32[1,6,64,64]{3,2,1,0:T(8,128)} %col_up.1) | copy-start | bytes 294916
  7.5 49.0 %all-to-all-start = ((bf16[256,8,128]{2,1,0:T(8,128)(2,1)}), bf16[256,8,128]{2,1,0:T(8,128)(2,1)S(1)}, u32[]{:S(2)}, u32[]{:S(2)}) async-start(bf16[256,8,128]{2,1,0:T(8,128)(2,1)} %get-tuple-element.14), calls=%async_computation | async-start | bytes 1048576 | tf_op jit(solution)/shard_map/all_to_all | solution.py:309
  22.0 28.3 %collective-permute-start = (bf16[8,1152]{1,0:T(8,128)(2,1)S(1)}, bf16[8,1152]{1,0:T(8,128)(2,1)S(1)}, u32[]{:S(2)}, u32[]{:S(2)}) collective-permute-start(bf16[8,1152]{1,0:T(8,128)(2,1)S(1)} %get-tuple-element.17), channel_id=1, source_target_pairs={{0,1},{1,2},{2,3},{3,4},{4,5},{5,6},{6,7},{7,8},{8,9},{9,10},{10,1... | collective-permute-start | bytes 55304 | tf_op jit(solution)/shard_map/ppermute | solution.py:310
  25.4 24.9 %collective-permute-start.1 = (bf16[8,1152]{1,0:T(8,128)(2,1)S(1)}, bf16[8,1152]{1,0:T(8,128)(2,1)S(1)}, u32[]{:S(2)}, u32[]{:S(2)}) collective-permute-start(bf16[8,1152]{1,0:T(8,128)(2,1)S(1)} %get-tuple-element.18), channel_id=1, source_target_pairs={{1,0},{2,1},{3,2},{4,3},{5,4},{6,5},{7,6},{8,7},{9,8},{10,9},{11,1... | collective-permute-start | bytes 55304 | tf_op jit(solution)/shard_map/ppermute | solution.py:311
  34.8 2.8 %copy-start = (bf16[16,3,256,256]{3,2,1,0:T(8,128)(2,1)S(1)}, bf16[16,3,256,256]{3,2,1,0:T(8,128)(2,1)}, u32[]{:S(2)}) copy-start(bf16[16,3,256,256]{3,2,1,0:T(8,128)(2,1)} %near_blocks.3) | copy-start | bytes 18874372
  37.6 1.2 %copy-start.2 = (f32[30,64,64]{2,1,0:T(8,128)S(1)}, f32[30,64,64]{2,1,0:T(8,128)}, u32[]{:S(2)}) copy-start(f32[30,64,64]{2,1,0:T(8,128)} %row_local.3) | copy-start | bytes 1474564
  38.8 1.2 %copy-start.6 = (f32[1,7,4,64,64]{4,3,2,1,0:T(8,128)S(1)}, f32[1,7,4,64,64]{4,3,2,1,0:T(8,128)}, u32[]{:S(2)}) copy-start(f32[1,7,4,64,64]{4,3,2,1,0:T(8,128)} %coupling.2) | copy-start | bytes 1376260
  40.0 0.8 %copy-start.8 = (bf16[8,4096]{1,0:T(8,128)(2,1)S(1)}, bf16[8,4096]{1,0:T(8,128)(2,1)}, u32[]{:S(2)}) copy-start(bf16[8,4096]{1,0:T(8,128)(2,1)} %rhs.5) | copy-start | bytes 196612
  40.8 0.9 %copy-start.12 = (f32[1,6,64,64]{3,2,1,0:T(8,128)S(1)}, f32[1,6,64,64]{3,2,1,0:T(8,128)}, u32[]{:S(2)}) copy-start(f32[1,6,64,64]{3,2,1,0:T(8,128)} %row_up.1) | copy-start | bytes 294916
  41.8 0.7 %copy-start.13 = (s32[16]{0:T(128)S(1)}, s32[16]{0:T(128)}, u32[]{:S(2)}) copy-start(s32[16]{0:T(128)} %count.4) | copy-start | bytes 196
  42.4 7.8 %copy-start.1 = (bf16[16,3,256,256]{3,2,1,0:T(8,128)(2,1)S(1)}, bf16[16,3,256,256]{3,2,1,0:T(8,128)(2,1)}, u32[]{:S(2)}) copy-start(bf16[16,3,256,256]{3,2,1,0:T(8,128)(2,1)} %near_blocks.3) | copy-start | bytes 18874372
  42.4 7.8 %copy-start.3 = (f32[30,64,64]{2,1,0:T(8,128)S(1)}, f32[30,64,64]{2,1,0:T(8,128)}, u32[]{:S(2)}) copy-start(f32[30,64,64]{2,1,0:T(8,128)} %row_local.3) | copy-start | bytes 1474564
  42.4 7.9 %copy-start.14 = (s32[28]{0:T(128)S(1)}, s32[28]{0:T(128)}, u32[]{:S(2)}) copy-start(s32[28]{0:T(128)} %local_count.1) | copy-start | bytes 340
  50.3 2.0 %copy-start.4 = (f32[28,4,64,64]{3,2,1,0:T(8,128)S(1)}, f32[28,4,64,64]{3,2,1,0:T(8,128)}, u32[]{:S(2)}) copy-start(f32[28,4,64,64]{3,2,1,0:T(8,128)} %coupling.3) | copy-start | bytes 5505028
  52.3 4.2 %copy-start.10 = (bf16[16,64,256]{2,1,0:T(8,128)(2,1)S(1)}, bf16[16,64,256]{2,1,0:T(8,128)(2,1)}, u32[]{:S(2)}) copy-start(bf16[16,64,256]{2,1,0:T(8,128)(2,1)} %row_basis.1) | copy-start | bytes 1572868
  52.3 4.2 %copy-start.15 = (s32[1,7]{1,0:T(1,128)S(1)}, s32[1,7]{1,0:T(1,128)}, u32[]{:S(2)}) copy-start(s32[1,7]{1,0:T(1,128)} %count.5) | copy-start | bytes 88

commit v2 on v1

v2 whole, which is shorter than its diff:
```python
import jax
import jax.numpy as jnp
from jax import lax
from jax.experimental import pallas as pl
from jax.experimental.pallas import tpu as pltpu
from jax.sharding import PartitionSpec as P

AXES = ("leaf", "slab")
F32 = jnp.float32
BF16 = jnp.bfloat16
LEAVES = 16
LEAF_LEN = 256
RANK = 64
NRHS = 8
TIERS = 7
SLOTS = 4
NDEV = 256
STARTS = (0, 16, 24, 28)
ROWS = (0, 16, 24)
EDGE = 2 * LEAF_LEN
HALO = EDGE + 10 * RANK
ZERO = 6
EARLY = 6


def mxu(left, right):
    return lax.dot_general(left, right, (((1,), (0,)), ((), ())), preferred_element_type=F32)


def mxu_t(left, right):
    return lax.dot_general(left, right, (((1,), (1,)), ((), ())), preferred_element_type=F32)


def split(value):
    high = value.astype(BF16)
    return high, (value - high.astype(F32)).astype(BF16)


def stacked(value):
    high = value.astype(BF16).astype(F32)
    return jnp.concatenate([high, value - high], axis=0).astype(BF16)


def folded(left, high, low):
    total = mxu(left, high) + mxu(left, low)
    half = total.shape[0] // 2
    return total[:half] + total[half:]


def product(left, right):
    return folded(stacked(left), *split(right))


def fetch(sources, targets, sems):
    copies = [
        pltpu.make_async_copy(source, target, sems.at[i])
        for i, (source, target) in enumerate(zip(sources, targets))
    ]
    for copy in copies:
        copy.start()
    return copies


def up_kernel(
    rhs_in,
    basis_in,
    local_in,
    up_in,
    near_in,
    blocks,
    coeffs,
    halo_first,
    halo_second,
    rhs,
    near_blocks,
    col_basis,
    col_local,
    col_up,
    sems,
    halo_up,
    halo_down,
):
    me = lax.axis_index("leaf") * 4 + lax.axis_index("slab")
    copies = fetch(
        (rhs_in, basis_in, local_in, up_in, near_in.at[pl.ds(2, EARLY)]),
        (rhs, col_basis, col_local, col_up, near_blocks),
        sems,
    )
    blocks[...] = jnp.zeros_like(blocks)
    copies[0].wait()
    copies[1].wait()
    level = [
        mxu_t(rhs[:, l * LEAF_LEN : (l + 1) * LEAF_LEN], col_basis[l]) for l in range(LEAVES)
    ]
    copies[2].wait()
    for h in range(4):
        width = LEAVES >> h
        if h < 3:
            for c in range(width):
                coeffs[ROWS[h] + c] = level[c]
            for i in range(3):
                at = EDGE + (h * 3 + i) * RANK
                halo_up[:, at : at + RANK] = level[width - 3 + i].astype(BF16)
                halo_down[:, at : at + RANK] = level[i].astype(BF16)
        above = []
        for j in range(width // 2):
            pair = jnp.concatenate([level[2 * j], level[2 * j + 1]], axis=1)
            moves = col_local[STARTS[h] + 2 * j : STARTS[h] + 2 * j + 2].reshape(2 * RANK, RANK)
            above.append(product(pair, moves))
        level = above
    halo_up[:, :EDGE] = rhs[:, (LEAVES - 2) * LEAF_LEN :]
    halo_down[:, :EDGE] = rhs[:, :EDGE]
    halo_up[:, HALO - RANK :] = jnp.zeros((NRHS, RANK), BF16)
    halo_down[:, HALO - RANK :] = jnp.zeros((NRHS, RANK), BF16)
    even = me % 2 == 0
    halo_first[...] = jnp.where(even, halo_up[...], halo_down[...])
    halo_second[...] = jnp.where(even, halo_down[...], halo_up[...])
    share = level[0]
    copies[3].wait()
    for u in range(TIERS):
        sent = share.astype(BF16)
        side = (u % 2) * RANK
        span = 1 << u
        own = lax.shift_right_logical(me, u)
        for off in (-3, -2, 2, 3):
            there = own + off

            @pl.when((there >= 0) & (there < (NDEV >> u)))
            def _():
                blocks[pl.ds(there * span, span), :, side : side + RANK] = jnp.broadcast_to(
                    sent[None], (span, NRHS, RANK)
                )

        if u < TIERS - 1:
            share = product(share, col_up[0, u])
    copies[4].wait()


def near_leaf(l, me, window, shift, blocks, partner, count):
    total = None
    for s in range(3):
        spot = partner[s, l] - me * LEAVES + shift
        part = window[:, pl.ds(pl.multiple_of(spot * LEAF_LEN, LEAF_LEN), LEAF_LEN)]
        if s == 2:
            part = jnp.where(count[l] > s, part, jnp.zeros_like(part))
        term = mxu_t(part, blocks[s])
        total = term if total is None else total + term
    return total


def inner_kernel(
    rhs,
    near_early,
    near_in,
    partner,
    count,
    coupling_in,
    local_in,
    near,
    paths,
    coupling,
    row_local,
    near_blocks,
    sems,
):
    me = lax.axis_index("leaf") * 4 + lax.axis_index("slab")
    late = LEAVES - 4 - EARLY
    copies = fetch(
        [local_in, coupling_in.at[pl.ds(LEAVES, 12)]]
        + [near_in.at[2 + EARLY + i] for i in range(late)],
        [row_local, coupling] + [near_blocks.at[i] for i in range(late)],
        sems,
    )
    for l in range(2, LEAVES - 2):
        i = l - 2 - EARLY
        if i >= 0:
            copies[2 + i].wait()
        near[:, (l - 2) * LEAF_LEN : (l - 1) * LEAF_LEN] = near_leaf(
            l, me, rhs, 0, near_early.at[l - 2] if i < 0 else near_blocks.at[i], partner, count
        )
    copies[0].wait()
    level = [row_local[STARTS[3] + c] for c in range(2)]
    for h in (2, 1, 0):
        level = [
            product(level[c // 2], row_local[STARTS[h] + c]) for c in range(LEAVES >> h)
        ]
    for l in range(LEAVES):
        high, low = split(level[l])
        paths[0, :, l * RANK : (l + 1) * RANK] = high
        paths[1, :, l * RANK : (l + 1) * RANK] = low
    copies[1].wait()


def edge_kernel(
    rhs,
    first,
    second,
    coeffs,
    near_in,
    partner,
    count,
    coupling_in,
    coupling_held,
    local_partner,
    local_count,
    row_local,
    up_in,
    pairs_in,
    basis_in,
    near,
    field,
    pairs,
    row_basis,
    coupling,
    row_up,
    up_coupling,
    near_blocks,
    sems,
    window,
    left,
    right,
):
    me = lax.axis_index("leaf") * 4 + lax.axis_index("slab")
    edges = (0, 1, LEAVES - 2, LEAVES - 1)
    copies = fetch(
        [coupling_in.at[pl.ds(0, LEAVES)]]
        + [near_in.at[l] for l in edges]
        + [pairs_in, up_in, basis_in],
        [coupling]
        + [near_blocks.at[i] for i in range(4)]
        + [up_coupling, row_up, row_basis],
        sems,
    )
    even = me % 2 == 0
    from_low = jnp.where(even, second[...], first[...])
    from_high = jnp.where(even, first[...], second[...])
    window[:, :EDGE] = from_low[:, :EDGE]
    window[:, EDGE : EDGE + LEAVES * LEAF_LEN] = rhs[...]
    window[:, EDGE + LEAVES * LEAF_LEN :] = from_high[:, :EDGE]
    blank = jnp.zeros((2 * NRHS, RANK), F32)

    def place(at, value):
        high = value.astype(BF16).astype(F32)
        both = jnp.concatenate([high, value - high], axis=0)
        left[at] = jnp.concatenate([both, blank], axis=1)
        right[at] = jnp.concatenate([blank, both], axis=1)

    bases = []
    base = 0
    for h in range(3):
        width = LEAVES >> h
        for i in range(3):
            at = EDGE + (h * 3 + i) * RANK
            place(base + i, from_low[:, at : at + RANK].astype(F32))
            place(base + 3 + width + i, from_high[:, at : at + RANK].astype(F32))
        for c in range(width):
            place(base + 3 + c, coeffs[ROWS[h] + c])
        left[base + width + ZERO] = jnp.zeros((2 * NRHS, 2 * RANK), F32)
        right[base + width + ZERO] = jnp.zeros((2 * NRHS, 2 * RANK), F32)
        bases.append(base)
        base += width + ZERO + 1

    def couple(h, c, matrices):
        row = ROWS[h] + c
        live = local_count[row]
        start = bases[h] + 3 - me * (LEAVES >> h)
        none = bases[h] + (LEAVES >> h) + ZERO
        spots = [
            jnp.where(s < live, local_partner[s, row] + start, none) for s in range(SLOTS)
        ]
        chosen = jnp.concatenate(
            [left[spots[0]] + right[spots[1]], left[spots[2]] + right[spots[3]]], axis=1
        ).astype(BF16)
        return folded(chosen, *split(matrices.reshape(SLOTS * RANK, RANK)))

    level = [couple(2, c, coupling_held[8 + c]) for c in range(4)]
    level = [
        couple(1, c, coupling_held[c]) + product(level[c // 2], row_local[STARTS[1] + c])
        for c in range(8)
    ]
    level = [product(level[c // 2], row_local[c]) for c in range(LEAVES)]
    copies[0].wait()
    for l in range(LEAVES):
        field[:, l * RANK : (l + 1) * RANK] = level[l] + couple(0, l, coupling[l])
    for i, l in enumerate(edges):
        copies[1 + i].wait()
        near[:, i * LEAF_LEN : (i + 1) * LEAF_LEN] = near_leaf(
            l, me, window, 2, near_blocks.at[i], partner, count
        )
    copies[5].wait()
    copies[6].wait()
    for u in range(TIERS):
        high, low = split(up_coupling[0, u].reshape(SLOTS * RANK, RANK))
        pairs[0, u * 256 : (u + 1) * 256] = high
        pairs[1, u * 256 : (u + 1) * 256] = low
    for u in range(TIERS - 1):
        high, low = split(row_up[0, u])
        at = TIERS * 256 + u * RANK
        pairs[0, at : at + RANK] = high
        pairs[1, at : at + RANK] = low
    copies[7].wait()


def final_kernel(
    got, partner, count, pairs, paths, field, near_inner, near_edge, row_basis, out
):
    lane = lax.broadcasted_iota(jnp.int32, (NRHS, 2 * RANK), 1)
    far = []
    for u in range(TIERS):
        span = 1 << u
        live = count[0, u]
        sums = []
        for s in range(SLOTS):
            block = got[pl.ds(partner[0, s, u] * span, span)].astype(F32)
            total = jnp.where(s < live, jnp.sum(block, axis=0), 0.0)
            sums.append(total if s % 2 == u % 2 else pltpu.roll(total, RANK, 1))
        chosen = jnp.concatenate(
            [
                jnp.where(lane < RANK, sums[0], sums[1]),
                jnp.where(lane < RANK, sums[2], sums[3]),
            ],
            axis=1,
        )
        rows = slice(u * 256, (u + 1) * 256)
        far.append(folded(stacked(chosen), pairs[0, rows], pairs[1, rows]))
    down = far[TIERS - 1]
    for u in reversed(range(TIERS - 1)):
        at = TIERS * 256 + u * RANK
        rows = slice(at, at + RANK)
        down = far[u] + folded(stacked(down), pairs[0, rows], pairs[1, rows])
    leaf_field = field[...] + folded(stacked(down), paths[0], paths[1])
    both = stacked(leaf_field)
    for l in range(LEAVES):
        total = mxu(both[:, l * RANK : (l + 1) * RANK], row_basis[l])
        if 2 <= l < LEAVES - 2:
            near = near_inner[:, (l - 2) * LEAF_LEN : (l - 1) * LEAF_LEN]
        else:
            i = l if l < 2 else l - (LEAVES - 4)
            near = near_edge[:, i * LEAF_LEN : (i + 1) * LEAF_LEN]
        out[:, l * LEAF_LEN : (l + 1) * LEAF_LEN] = near + total[:NRHS] + total[NRHS:]


VMEM = pl.BlockSpec(memory_space=pltpu.VMEM)
SMEM = pl.BlockSpec(memory_space=pltpu.SMEM)
HBM = pl.BlockSpec(memory_space=pltpu.HBM)


def held(shape, dtype):
    return pltpu.VMEM(shape, dtype)


def far_away(value):
    return pltpu.with_memory_space_constraint(value, pltpu.HBM)


LIMIT = pltpu.CompilerParams(vmem_limit_bytes=32 * 1024 * 1024)


def cost(flops, size):
    return pl.CostEstimate(flops=flops, bytes_accessed=size, transcendentals=0)


def body(
    rhs,
    col_basis,
    row_basis,
    near_blocks,
    near_partner,
    near_count,
    col_transfer_local,
    row_transfer_local,
    local_coupling,
    local_partner,
    local_count,
    col_transfer_up,
    row_transfer_up,
    up_coupling,
    up_partner,
    up_count,
):
    shape = jax.ShapeDtypeStruct
    blocks, coeffs, halo_first, halo_second, rhs_held, near_held = pl.pallas_call(
        up_kernel,
        out_shape=(
            shape((NDEV, NRHS, 2 * RANK), BF16),
            held((28, NRHS, RANK), F32),
            held((NRHS, HALO), BF16),
            held((NRHS, HALO), BF16),
            held(rhs.shape, BF16),
            held((EARLY,) + near_blocks.shape[1:], BF16),
        ),
        in_specs=[HBM] * 5,
        out_specs=(VMEM,) * 6,
        scratch_shapes=[
            pltpu.VMEM(col_basis.shape, BF16),
            pltpu.VMEM(col_transfer_local.shape, F32),
            pltpu.VMEM(col_transfer_up.shape, F32),
            pltpu.SemaphoreType.DMA((5,)),
            pltpu.VMEM((NRHS, HALO), BF16),
            pltpu.VMEM((NRHS, HALO), BF16),
        ],
        compiler_params=LIMIT,
        cost_estimate=cost(2 * 10**7, 10**7),
    )(*map(far_away, (rhs, col_basis, col_transfer_local, col_transfer_up, near_blocks)))
    firsts = [(i, i ^ 1) for i in range(NDEV)]
    seconds = [(i, ((i + 1) ^ 1) - 1) for i in range(1, NDEV - 1)]
    got = lax.all_to_all(blocks, AXES, 0, 0)
    first = lax.ppermute(halo_first, AXES, firsts)
    second = lax.ppermute(halo_second, AXES, seconds)
    partner = near_partner.T
    near_inner, paths, coupling_held, local_held = pl.pallas_call(
        inner_kernel,
        out_shape=(
            held((NRHS, (LEAVES - 4) * LEAF_LEN), F32),
            held((2, RANK, LEAVES * RANK), BF16),
            held((12,) + local_coupling.shape[1:], F32),
            held(row_transfer_local.shape, F32),
        ),
        in_specs=[VMEM, VMEM, HBM, SMEM, SMEM, HBM, HBM],
        out_specs=(VMEM,) * 4,
        scratch_shapes=[
            pltpu.VMEM((LEAVES - 4 - EARLY,) + near_blocks.shape[1:], BF16),
            pltpu.SemaphoreType.DMA((LEAVES - 2 - EARLY,)),
        ],
        compiler_params=LIMIT,
        cost_estimate=cost(2 * 10**8, 10**7),
    )(
        rhs_held,
        near_held,
        far_away(near_blocks),
        partner,
        near_count,
        far_away(local_coupling),
        far_away(row_transfer_local),
    )
    entries = 28 + 3 * (ZERO + 1)
    near_edge, field, pairs, basis_held = pl.pallas_call(
        edge_kernel,
        out_shape=(
            held((NRHS, 4 * LEAF_LEN), F32),
            held((NRHS, LEAVES * RANK), F32),
            held((2, TIERS * 256 + (TIERS - 1) * RANK, RANK), BF16),
            held(row_basis.shape, BF16),
        ),
        in_specs=[VMEM] * 4 + [HBM, SMEM, SMEM, HBM, VMEM, SMEM, SMEM, VMEM] + [HBM] * 3,
        out_specs=(VMEM,) * 4,
        scratch_shapes=[
            pltpu.VMEM((LEAVES,) + local_coupling.shape[1:], F32),
            pltpu.VMEM(row_transfer_up.shape, F32),
            pltpu.VMEM(up_coupling.shape, F32),
            pltpu.VMEM((4,) + near_blocks.shape[1:], BF16),
            pltpu.SemaphoreType.DMA((8,)),
            pltpu.VMEM((NRHS, LEAVES * LEAF_LEN + 2 * EDGE), BF16),
            pltpu.VMEM((entries, 2 * NRHS, 2 * RANK), F32),
            pltpu.VMEM((entries, 2 * NRHS, 2 * RANK), F32),
        ],
        compiler_params=LIMIT,
        cost_estimate=cost(10**8, 5 * 10**6),
    )(
        rhs_held,
        first,
        second,
        coeffs,
        far_away(near_blocks),
        partner,
        near_count,
        far_away(local_coupling),
        coupling_held,
        local_partner.T,
        local_count,
        local_held,
        *map(far_away, (row_transfer_up, up_coupling, row_basis)),
    )
    return pl.pallas_call(
        final_kernel,
        out_shape=shape((NRHS, LEAVES * LEAF_LEN), F32),
        in_specs=[VMEM, SMEM, SMEM] + [VMEM] * 6,
        out_specs=VMEM,
        compiler_params=LIMIT,
        cost_estimate=cost(2 * 10**7, 3 * 10**6),
    )(
        got,
        up_partner.transpose(0, 2, 1),
        up_count,
        pairs,
        paths,
        field,
        near_inner,
        near_edge,
        basis_held,
    )


def solution(mesh):
    return jax.shard_map(
        body,
        mesh=mesh,
        in_specs=(
            P(None, AXES),
            P(AXES, None, None),
            P(AXES, None, None),
            P(AXES, None, None, None),
            P(AXES, None),
            P(AXES),
            P(AXES, None, None),
            P(AXES, None, None),
            P(AXES, None, None, None),
            P(AXES, None),
            P(AXES),
            P(AXES, None, None, None),
            P(AXES, None, None, None),
            P(AXES, None, None, None, None),
            P(AXES, None, None),
            P(AXES, None),
        ),
        out_specs=P(None, AXES),
        check_vma=False,
    )
```

time: 60 us -> 44.9 us (0.75)
  the two profiles are of different devices: /device:TPU:24 before, /device:TPU:1 now
where the time goes in v2:
time: 44.9 us; the launch traced here: 44.7 us
  starting transfers between devices  21.6 us (48%)
  Pallas kernels  17.7 us (39%)
  waiting for transfers between devices  5.24 us (12%)
    all_to_all x1, starting transfers between devices, body(): got = lax.all_to_all(blocks, AXES, 0, 0)  15.9 us
    pallas_call x1, Pallas kernels, body(): pl.pallas_call(inner_kernel, out_shape=(held((NRHS, (LEAVES - 4) * LEAF_L...  5.55 us
    all_to_all x1, waiting for transfers between devices, body(): got = lax.all_to_all(blocks, AXES, 0, 0)  5.24 us
    pallas_call x1, Pallas kernels, body(): pl.pallas_call(edge_kernel, out_shape=(held((NRHS, 4 * LEAF_LEN), F32), h...  4.83 us
    pallas_call x1, Pallas kernels, body(): pl.pallas_call(up_kernel, out_shape=(shape((NDEV, NRHS, 2 * RANK), BF16),...  4.56 us
    ppermute x1, starting transfers between devices, body(): second = lax.ppermute(halo_second, AXES, seconds)  4.21 us
    pallas_call x1, Pallas kernels, body(): pl.pallas_call(final_kernel, out_shape=shape((NRHS, LEAVES * LEAF_LEN), F...  2.75 us
    ppermute x1, starting transfers between devices, body(): first = lax.ppermute(halo_first, AXES, firsts)  1.47 us
  transfers between devices with their start and end apart: 3, of which 1 were waited for; matrix products, arithmetic and copies ran while one was open for 0% of the time, Pallas kernels for 23%

profile of v2, /device:TPU:1, one launch (start us, length us, event | category | flops | bytes accessed | tf_op | source)
XLA Modules:
  0.0 44.7 jit_solution(5911912679636003609)
XLA Ops:
  0.0 0.0 copy-start.3
  0.0 0.0 copy-start
  0.0 4.6 %shard_map.154 = (bf16[256,8,128]{2,1,0:T(8,128)(2,1)}, f32[28,8,64]{2,1,0:T(8,128)S(1)}, bf16[8,1152]{1,0:T(8,128)(2,1)S(1)}, bf16[8,1152]{1,0:T(8,128)(2,1)S(1...) custom-call(bf16[8,4096]{1,0:T(8,128)(2,1)} %rhs_in.1, bf16[16,64,256]{2,1,0:T(8,128)(2,1)} %basis_in.2, ...), custom_call_target="tpu_custom_call" | custom-call | flops 20000000 | bytes 10000000 | tf_op jit(solution)/shard_map/pallas_call | solution.py:382
  4.6 15.9 %all-to-all-start = ((bf16[256,8,128]{2,1,0:T(8,128)(2,1)}), bf16[256,8,128]{2,1,0:T(8,128)(2,1)S(1)}, u32[]{:S(2)}, u32[]{:S(2)}) async-start(bf16[256,8,128]{2,1,0:T(8,128)(2,1)} %get-tuple-element.19), calls=%async_computation | async-start | bytes 1048576 | tf_op jit(solution)/shard_map/all_to_all | solution.py:407
  20.5 1.5 %collective-permute-start = (bf16[8,1152]{1,0:T(8,128)(2,1)S(1)}, bf16[8,1152]{1,0:T(8,128)(2,1)S(1)}, u32[]{:S(2)}, u32[]{:S(2)}) collective-permute-start(bf16[8,1152]{1,0:T(8,128)(2,1)S(1)} %get-tuple-element.21), channel_id=1, source_target_pairs={{0,1},{1,0},{2,3},{3,2},{4,5},{5,4},{6,7},{7,6},{8,9},{9,8},{10,11... | collective-permute-start | bytes 55304 | tf_op jit(solution)/shard_map/ppermute | solution.py:408
  22.0 4.2 %collective-permute-start.1 = (bf16[8,1152]{1,0:T(8,128)(2,1)S(1)}, bf16[8,1152]{1,0:T(8,128)(2,1)S(1)}, u32[]{:S(2)}, u32[]{:S(2)}) collective-permute-start(bf16[8,1152]{1,0:T(8,128)(2,1)S(1)} %get-tuple-element.22), channel_id=1, source_target_pairs={{1,2},{2,1},{3,4},{4,3},{5,6},{6,5},{7,8},{8,7},{9,10},{10,9},{11,... | collective-permute-start | bytes 55304 | tf_op jit(solution)/shard_map/ppermute | solution.py:409
  26.2 0.0 copy-done.3
  26.2 0.0 copy-done
  26.2 0.0 copy-start.1
  26.3 0.0 copy-start.4
  26.3 5.6 %shard_map.155 = (f32[8,3072]{1,0:T(8,128)S(1)}, bf16[2,64,1024]{2,1,0:T(8,128)(2,1)S(1)}, f32[12,4,64,64]{3,2,1,0:T(8,128)S(1)}, f32[30,64,64]{2,1,0:T(8,128)S(1)}) custom-call(bf16[8,4096]{1,0:T(8,128)(2,1)S(1)} %get-tuple-element.20.rhs, bf16[6,3,256,256]{3,2,1,0:T(8,128)(2,1)S(1)} %get-tuple-element.24.near_early, bf16[16,3,256,256]{3,2,1,0:T(8,128)(2,1)} %near_in.5, ...), custom_call_target="tpu_custom_call" | custom-call | flops 200000000 | bytes 10000000 | tf_op jit(solution)/shard_map/pallas_call | solution.py:411
  31.8 0.0 collective-permute-done.first
  31.8 0.0 collective-permute-done.1.second
  31.8 0.0 copy-done.1
  31.9 0.0 copy-done.4
  31.9 0.0 copy-start.2
  31.9 0.0 copy-start.5
  31.9 4.8 %shard_map.156 = (f32[8,1024]{1,0:T(8,128)S(1)}, f32[8,1024]{1,0:T(8,128)S(1)}, bf16[2,2176,64]{2,1,0:T(8,128)(2,1)S(1)}, bf16[16,64,256]{2,1,0:T(8,128)(2,1)S(1)}) custom-call(bf16[8,4096]{1,0:T(8,128)(2,1)S(1)} %get-tuple-element.20.rhs, bf16[8,1152]{1,0:T(8,128)(2,1)S(1)} %collective-permute-done.first, ...), custom_call_target="tpu_custom_call" | custom-call | flops 100000000 | bytes 5000000 | tf_op jit(solution)/shard_map/pallas_call | solution.py:437
  36.7 5.2 %all-to-all-done.got = bf16[256,8,128]{2,1,0:T(8,128)(2,1)S(1)} async-done(((bf16[256,8,128]{2,1,0:T(8,128)(2,1)}), bf16[256,8,128]{2,1,0:T(8,128)(2,1)S(1)}, u32[]{:S(2)}, u32[]{:S(2)}) %all-to-all-start) | async-done | bytes 524320 | tf_op jit(solution)/shard_map/all_to_all | solution.py:407
  42.0 0.0 copy-done.2
  42.0 0.0 copy-done.5
  42.0 2.8 %shard_map.157 = f32[8,4096]{1,0:T(8,128)} custom-call(bf16[256,8,128]{2,1,0:T(8,128)(2,1)S(1)} %all-to-all-done.got, s32[1,4,7]{2,1,0:T(4,128)S(1)} %bitcast.6, s32[1,7]{1,0:T(1,128)S(1)} %copy-done.5, bf16[2,2176,64]{2,1,0:T(8,128)(2,1)S(1)} %get-tuple-element.27.pairs, bf16[2,64,1024]{2,1,0:T(8,128)(2,1)S(1)} %get-tuple-element.28.paths, ...), custom_call_target="tpu_custom_call" | custom-call | flops 20000000 | bytes 3000000 | tf_op jit(solution)/shard_map/pallas_call | solution.py:474
Async XLA Ops:
  0.0 26.2 %copy-start.3 = (s32[16]{0:T(128)S(1)}, s32[16]{0:T(128)}, u32[]{:S(2)}) copy-start(s32[16]{0:T(128)} %count.4) | copy-start | bytes 196
  0.0 26.2 %copy-start = (s32[16,3]{0,1:T(4,128)S(1)}, s32[16,3]{0,1:T(4,128)}, u32[]{:S(2)}) copy-start(s32[16,3]{0,1:T(4,128)} %param.20) | copy-start | bytes 580
  4.6 37.4 %all-to-all-start = ((bf16[256,8,128]{2,1,0:T(8,128)(2,1)}), bf16[256,8,128]{2,1,0:T(8,128)(2,1)S(1)}, u32[]{:S(2)}, u32[]{:S(2)}) async-start(bf16[256,8,128]{2,1,0:T(8,128)(2,1)} %get-tuple-element.19), calls=%async_computation | async-start | bytes 1048576 | tf_op jit(solution)/shard_map/all_to_all | solution.py:407
  20.5 11.3 %collective-permute-start = (bf16[8,1152]{1,0:T(8,128)(2,1)S(1)}, bf16[8,1152]{1,0:T(8,128)(2,1)S(1)}, u32[]{:S(2)}, u32[]{:S(2)}) collective-permute-start(bf16[8,1152]{1,0:T(8,128)(2,1)S(1)} %get-tuple-element.21), channel_id=1, source_target_pairs={{0,1},{1,0},{2,3},{3,2},{4,5},{5,4},{6,7},{7,6},{8,9},{9,8},{10,11... | collective-permute-start | bytes 55304 | tf_op jit(solution)/shard_map/ppermute | solution.py:408
  22.0 9.8 %collective-permute-start.1 = (bf16[8,1152]{1,0:T(8,128)(2,1)S(1)}, bf16[8,1152]{1,0:T(8,128)(2,1)S(1)}, u32[]{:S(2)}, u32[]{:S(2)}) collective-permute-start(bf16[8,1152]{1,0:T(8,128)(2,1)S(1)} %get-tuple-element.22), channel_id=1, source_target_pairs={{1,2},{2,1},{3,4},{4,3},{5,6},{6,5},{7,8},{8,7},{9,10},{10,9},{11,... | collective-permute-start | bytes 55304 | tf_op jit(solution)/shard_map/ppermute | solution.py:409
  26.2 5.6 %copy-start.1 = (s32[28,4]{0,1:T(4,128)S(1)}, s32[28,4]{0,1:T(4,128)}, u32[]{:S(2)}) copy-start(s32[28,4]{0,1:T(4,128)} %param.25) | copy-start | bytes 1348
  26.3 5.6 %copy-start.4 = (s32[28]{0:T(128)S(1)}, s32[28]{0:T(128)}, u32[]{:S(2)}) copy-start(s32[28]{0:T(128)} %local_count.1) | copy-start | bytes 340
  31.9 10.1 %copy-start.2 = (s32[1,7,4]{1,2,0:T(4,128)S(1)}, s32[1,7,4]{1,2,0:T(4,128)}, u32[]{:S(2)}) copy-start(s32[1,7,4]{1,2,0:T(4,128)} %param.30) | copy-start | bytes 340
  31.9 10.1 %copy-start.5 = (s32[1,7]{1,0:T(1,128)S(1)}, s32[1,7]{1,0:T(1,128)}, u32[]{:S(2)}) copy-start(s32[1,7]{1,0:T(1,128)} %count.5) | copy-start | bytes 88

commit v3 on v2

--- a/solution.py
+++ b/solution.py
@@ -15,6 +15,7 @@
 TIERS = 7
 SLOTS = 4
 NDEV = 256
+BOXES = (8, 4, 4, 2)
 STARTS = (0, 16, 24, 28)
 ROWS = (0, 16, 24)
 EDGE = 2 * LEAF_LEN
@@ -59,6 +60,30 @@
     for copy in copies:
         copy.start()
     return copies
+
+
+def box(tier, cluster):
+    first = cluster * (1 << tier)
+    z = lax.shift_right_logical(first, 3) & 7
+    y = lax.shift_right_logical(first, 6)
+    x = first & 3
+    core = lax.shift_right_logical(first, 2) & 1
+    return (
+        pl.ds(z, 1 << max(tier - 3, 0)),
+        pl.ds(y, 1),
+        pl.ds(x, 1 << min(tier, 2)),
+        pl.ds(core, 2 if tier > 2 else 1),
+    )
+
+
+def exchange_order():
+    return [
+        ((y * 8 + z) * 2 + core) * 4 + x
+        for z in range(8)
+        for y in range(4)
+        for x in range(4)
+        for core in range(2)
+    ]
 
 
 def up_kernel(
@@ -115,24 +140,23 @@
     even = me % 2 == 0
     halo_first[...] = jnp.where(even, halo_up[...], halo_down[...])
     halo_second[...] = jnp.where(even, halo_down[...], halo_up[...])
+    copies[3].wait()
     share = level[0]
-    copies[3].wait()
-    for u in range(TIERS):
-        sent = share.astype(BF16)
+    sent = [share.astype(BF16)]
+    for u in range(TIERS - 1):
+        share = product(share, col_up[0, u])
+        sent.append(share.astype(BF16))
+    for u in reversed(range(TIERS)):
         side = (u % 2) * RANK
-        span = 1 << u
         own = lax.shift_right_logical(me, u)
         for off in (-3, -2, 2, 3):
             there = own + off
-
-            @pl.when((there >= 0) & (there < (NDEV >> u)))
-            def _():
-                blocks[pl.ds(there * span, span), :, side : side + RANK] = jnp.broadcast_to(
-                    sent[None], (span, NRHS, RANK)
-                )
-
-        if u < TIERS - 1:
-            share = product(share, col_up[0, u])
+            there = jnp.where((there >= 0) & (there < (NDEV >> u)), there, own)
+            place = box(u, there)
+            sizes = tuple(part.size for part in place)
+            blocks[(*place, slice(None), slice(side, side + RANK))] = jnp.broadcast_to(
+                sent[u], sizes + (NRHS, RANK)
+            )
     copies[4].wait()
 
 
@@ -307,12 +331,12 @@
     lane = lax.broadcasted_iota(jnp.int32, (NRHS, 2 * RANK), 1)
     far = []
     for u in range(TIERS):
-        span = 1 << u
         live = count[0, u]
         sums = []
         for s in range(SLOTS):
-            block = got[pl.ds(partner[0, s, u] * span, span)].astype(F32)
-            total = jnp.where(s < live, jnp.sum(block, axis=0), 0.0)
+            block = got[box(u, partner[0, s, u])].astype(F32)
+            total = jnp.sum(block.reshape(1 << u, NRHS, 2 * RANK), axis=0)
+            total = jnp.where(s < live, total, 0.0)
             sums.append(total if s % 2 == u % 2 else pltpu.roll(total, RANK, 1))
         chosen = jnp.concatenate(
             [
@@ -382,7 +406,7 @@
     blocks, coeffs, halo_first, halo_second, rhs_held, near_held = pl.pallas_call(
         up_kernel,
         out_shape=(
-            shape((NDEV, NRHS, 2 * RANK), BF16),
+            shape(BOXES + (NRHS, 2 * RANK), BF16),
             held((28, NRHS, RANK), F32),
             held((NRHS, HALO), BF16),
             held((NRHS, HALO), BF16),
@@ -404,7 +428,13 @@
     )(*map(far_away, (rhs, col_basis, col_transfer_local, col_transfer_up, near_blocks)))
     firsts = [(i, i ^ 1) for i in range(NDEV)]
     seconds = [(i, ((i + 1) ^ 1) - 1) for i in range(1, NDEV - 1)]
-    got = lax.all_to_all(blocks, AXES, 0, 0)
+    got = lax.all_to_all(
+        blocks.reshape(NDEV, NRHS, 2 * RANK),
+        AXES,
+        0,
+        0,
+        axis_index_groups=[exchange_order()],
+    ).reshape(BOXES + (NRHS, 2 * RANK))
     first = lax.ppermute(halo_first, AXES, firsts)
     second = lax.ppermute(halo_second, AXES, seconds)
     partner = near_partner.T

time: 44.9 us -> 42.7 us (0.951)
  waiting for transfers between devices: 5.24 us -> 3.69 us
    all_to_all x1, waiting for transfers between devices: 5.24 us -> 3.69 us  [body(): lax.all_to_all(blocks.reshape(NDEV, NRHS, 2 * RANK), AXES, 0, 0, axis_ind...]
  transfers between devices with their start and end apart: 3 -> 3, of which waited for: 1 -> 1; matrix products, arithmetic and copies ran while one was open for 0% -> 0% of each run, Pallas kernels for 23% -> 24%
where the time goes in v3:
time: 42.7 us; the launch traced here: 42.5 us
  starting transfers between devices  21.3 us (50%)
  Pallas kernels  17.3 us (41%)
  waiting for transfers between devices  3.69 us (9%)
    all_to_all x1, starting transfers between devices, body(): lax.all_to_all(blocks.reshape(NDEV, NRHS, 2 * RANK), AXES, 0, 0, axis_ind...  15.7 us
    pallas_call x1, Pallas kernels, body(): pl.pallas_call(inner_kernel, out_shape=(held((NRHS, (LEAVES - 4) * LEAF_L...  5.55 us
    pallas_call x1, Pallas kernels, body(): pl.pallas_call(edge_kernel, out_shape=(held((NRHS, 4 * LEAF_LEN), F32), h...  4.83 us
    ppermute x1, starting transfers between devices, body(): second = lax.ppermute(halo_second, AXES, seconds)  4.21 us
    pallas_call x1, Pallas kernels, body(): pl.pallas_call(up_kernel, out_shape=(shape(BOXES + (NRHS, 2 * RANK), BF16...  4.15 us
    all_to_all x1, waiting for transfers between devices, body(): lax.all_to_all(blocks.reshape(NDEV, NRHS, 2 * RANK), AXES, 0, 0, axis_ind...  3.69 us
    pallas_call x1, Pallas kernels, body(): pl.pallas_call(final_kernel, out_shape=shape((NRHS, LEAVES * LEAF_LEN), F...  2.77 us
    ppermute x1, starting transfers between devices, body(): first = lax.ppermute(halo_first, AXES, firsts)  1.47 us
  transfers between devices with their start and end apart: 3, of which 1 were waited for; matrix products, arithmetic and copies ran while one was open for 0% of the time, Pallas kernels for 24%

profile of v3, /device:TPU:1, one launch (start us, length us, event | category | flops | bytes accessed | tf_op | source)
XLA Modules:
  0.0 42.5 jit_solution(14239167333990529952)
XLA Ops:
  0.0 0.0 copy-start.3
  0.0 0.0 copy-start
  0.0 4.1 %shard_map.154 = (bf16[8,4,4,2,8,128]{5,4,3,2,1,0:T(8,128)(2,1)}, f32[28,8,64]{2,1,0:T(8,128)S(1)}, bf16[8,1152]{1,0:T(8,128)(2,1)S(1)}, bf16[8,1152]{1,0:T(8,12...) custom-call(bf16[8,4096]{1,0:T(8,128)(2,1)} %rhs_in.1, bf16[16,64,256]{2,1,0:T(8,128)(2,1)} %basis_in.2, ...), custom_call_target="tpu_custom_call" | custom-call | flops 20000000 | bytes 10000000 | tf_op jit(solution)/shard_map/pallas_call | solution.py:406
  4.2 15.7 %all-to-all-start = ((bf16[256,8,128]{2,1,0:T(8,128)(2,1)}), bf16[256,8,128]{2,1,0:T(8,128)(2,1)S(1)}, u32[]{:S(2)}, u32[]{:S(2)}) async-start(bf16[256,8,128]{2,1,0:T(8,128)(2,1)} %bitcast), calls=%async_computation | async-start | bytes 1048576 | tf_op jit(solution)/shard_map/all_to_all | solution.py:431
  19.8 1.5 %collective-permute-start = (bf16[8,1152]{1,0:T(8,128)(2,1)S(1)}, bf16[8,1152]{1,0:T(8,128)(2,1)S(1)}, u32[]{:S(2)}, u32[]{:S(2)}) collective-permute-start(bf16[8,1152]{1,0:T(8,128)(2,1)S(1)} %get-tuple-element.21), channel_id=1, source_target_pairs={{0,1},{1,0},{2,3},{3,2},{4,5},{5,4},{6,7},{7,6},{8,9},{9,8},{10,11... | collective-permute-start | bytes 55304 | tf_op jit(solution)/shard_map/ppermute | solution.py:438
  21.3 4.2 %collective-permute-start.1 = (bf16[8,1152]{1,0:T(8,128)(2,1)S(1)}, bf16[8,1152]{1,0:T(8,128)(2,1)S(1)}, u32[]{:S(2)}, u32[]{:S(2)}) collective-permute-start(bf16[8,1152]{1,0:T(8,128)(2,1)S(1)} %get-tuple-element.22), channel_id=1, source_target_pairs={{1,2},{2,1},{3,4},{4,3},{5,6},{6,5},{7,8},{8,7},{9,10},{10,9},{11,... | collective-permute-start | bytes 55304 | tf_op jit(solution)/shard_map/ppermute | solution.py:439
  25.5 0.0 copy-done.3
  25.5 0.0 copy-done
  25.5 0.0 copy-start.1
  25.6 0.0 copy-start.4
  25.6 5.6 %shard_map.155 = (f32[8,3072]{1,0:T(8,128)S(1)}, bf16[2,64,1024]{2,1,0:T(8,128)(2,1)S(1)}, f32[12,4,64,64]{3,2,1,0:T(8,128)S(1)}, f32[30,64,64]{2,1,0:T(8,128)S(1)}) custom-call(bf16[8,4096]{1,0:T(8,128)(2,1)S(1)} %get-tuple-element.20.rhs, bf16[6,3,256,256]{3,2,1,0:T(8,128)(2,1)S(1)} %get-tuple-element.24.near_early, bf16[16,3,256,256]{3,2,1,0:T(8,128)(2,1)} %near_in.5, ...), custom_call_target="tpu_custom_call" | custom-call | flops 200000000 | bytes 10000000 | tf_op jit(solution)/shard_map/pallas_call | solution.py:441
  31.1 0.0 collective-permute-done.first
  31.1 0.0 collective-permute-done.1.second
  31.2 0.0 copy-done.1
  31.2 0.0 copy-done.4
  31.2 0.0 copy-start.2
  31.2 0.0 copy-start.5
  31.2 4.8 %shard_map.156 = (f32[8,1024]{1,0:T(8,128)S(1)}, f32[8,1024]{1,0:T(8,128)S(1)}, bf16[2,2176,64]{2,1,0:T(8,128)(2,1)S(1)}, bf16[16,64,256]{2,1,0:T(8,128)(2,1)S(1)}) custom-call(bf16[8,4096]{1,0:T(8,128)(2,1)S(1)} %get-tuple-element.20.rhs, bf16[8,1152]{1,0:T(8,128)(2,1)S(1)} %collective-permute-done.first, ...), custom_call_target="tpu_custom_call" | custom-call | flops 100000000 | bytes 5000000 | tf_op jit(solution)/shard_map/pallas_call | solution.py:467
  36.0 3.7 %all-to-all-done = bf16[256,8,128]{2,1,0:T(8,128)(2,1)S(1)} async-done(((bf16[256,8,128]{2,1,0:T(8,128)(2,1)}), bf16[256,8,128]{2,1,0:T(8,128)(2,1)S(1)}, u32[]{:S(2)}, u32[]{:S(2)}) %all-to-all-start) | async-done | bytes 524320 | tf_op jit(solution)/shard_map/all_to_all | solution.py:431
  39.7 0.0 copy-done.2
  39.7 0.0 copy-done.5
  39.7 2.8 %shard_map.157 = f32[8,4096]{1,0:T(8,128)} custom-call(bf16[8,4,4,2,8,128]{5,4,3,2,1,0:T(8,128)(2,1)S(1)} %bitcast.5, s32[1,4,7]{2,1,0:T(4,128)S(1)} %bitcast.9, s32[1,7]{1,0:T(1,128)S(1)} %copy-done.5, bf16[2,2176,64]{2,1,0:T(8,128)(2,1)S(1)} %get-tuple-element.27.pairs, bf16[2,64,1024]{2,1,0:T(8,128)(2,1)S(1)} %get-tuple-element.28.paths, ...), custom_call_target="tpu_custom_call" | custom-call | flops 20000000 | bytes 3000000 | tf_op jit(solution)/shard_map/pallas_call | solution.py:504
Async XLA Ops:
  0.0 25.5 %copy-start.3 = (s32[16]{0:T(128)S(1)}, s32[16]{0:T(128)}, u32[]{:S(2)}) copy-start(s32[16]{0:T(128)} %count.4) | copy-start | bytes 196
  0.0 25.5 %copy-start = (s32[16,3]{0,1:T(4,128)S(1)}, s32[16,3]{0,1:T(4,128)}, u32[]{:S(2)}) copy-start(s32[16,3]{0,1:T(4,128)} %param.20) | copy-start | bytes 580
  4.2 35.6 %all-to-all-start = ((bf16[256,8,128]{2,1,0:T(8,128)(2,1)}), bf16[256,8,128]{2,1,0:T(8,128)(2,1)S(1)}, u32[]{:S(2)}, u32[]{:S(2)}) async-start(bf16[256,8,128]{2,1,0:T(8,128)(2,1)} %bitcast), calls=%async_computation | async-start | bytes 1048576 | tf_op jit(solution)/shard_map/all_to_all | solution.py:431
  19.8 11.3 %collective-permute-start = (bf16[8,1152]{1,0:T(8,128)(2,1)S(1)}, bf16[8,1152]{1,0:T(8,128)(2,1)S(1)}, u32[]{:S(2)}, u32[]{:S(2)}) collective-permute-start(bf16[8,1152]{1,0:T(8,128)(2,1)S(1)} %get-tuple-element.21), channel_id=1, source_target_pairs={{0,1},{1,0},{2,3},{3,2},{4,5},{5,4},{6,7},{7,6},{8,9},{9,8},{10,11... | collective-permute-start | bytes 55304 | tf_op jit(solution)/shard_map/ppermute | solution.py:438
  21.3 9.8 %collective-permute-start.1 = (bf16[8,1152]{1,0:T(8,128)(2,1)S(1)}, bf16[8,1152]{1,0:T(8,128)(2,1)S(1)}, u32[]{:S(2)}, u32[]{:S(2)}) collective-permute-start(bf16[8,1152]{1,0:T(8,128)(2,1)S(1)} %get-tuple-element.22), channel_id=1, source_target_pairs={{1,2},{2,1},{3,4},{4,3},{5,6},{6,5},{7,8},{8,7},{9,10},{10,9},{11,... | collective-permute-start | bytes 55304 | tf_op jit(solution)/shard_map/ppermute | solution.py:439
  25.5 5.6 %copy-start.1 = (s32[28,4]{0,1:T(4,128)S(1)}, s32[28,4]{0,1:T(4,128)}, u32[]{:S(2)}) copy-start(s32[28,4]{0,1:T(4,128)} %param.25) | copy-start | bytes 1348
  25.6 5.6 %copy-start.4 = (s32[28]{0:T(128)S(1)}, s32[28]{0:T(128)}, u32[]{:S(2)}) copy-start(s32[28]{0:T(128)} %local_count.1) | copy-start | bytes 340
  31.2 8.5 %copy-start.2 = (s32[1,7,4]{1,2,0:T(4,128)S(1)}, s32[1,7,4]{1,2,0:T(4,128)}, u32[]{:S(2)}) copy-start(s32[1,7,4]{1,2,0:T(4,128)} %param.30) | copy-start | bytes 340
  31.2 8.5 %copy-start.5 = (s32[1,7]{1,0:T(1,128)S(1)}, s32[1,7]{1,0:T(1,128)}, u32[]{:S(2)}) copy-start(s32[1,7]{1,0:T(1,128)} %count.5) | copy-start | bytes 88

commit v4 on v3

--- a/solution.py
+++ b/solution.py
@@ -22,6 +22,7 @@
 HALO = EDGE + 10 * RANK
 ZERO = 6
 EARLY = 6
+PIECE = 4
 
 
 def mxu(left, right):
@@ -326,7 +327,7 @@
 
 
 def final_kernel(
-    got, partner, count, pairs, paths, field, near_inner, near_edge, row_basis, out
+    got, partner, count, pairs, paths, field, near_inner, near_edge, row_basis, out, staged, sems
 ):
     lane = lax.broadcasted_iota(jnp.int32, (NRHS, 2 * RANK), 1)
     far = []
@@ -354,6 +355,7 @@
         down = far[u] + folded(stacked(down), pairs[0, rows], pairs[1, rows])
     leaf_field = field[...] + folded(stacked(down), paths[0], paths[1])
     both = stacked(leaf_field)
+    copies = []
     for l in range(LEAVES):
         total = mxu(both[:, l * RANK : (l + 1) * RANK], row_basis[l])
         if 2 <= l < LEAVES - 2:
@@ -361,7 +363,14 @@
         else:
             i = l if l < 2 else l - (LEAVES - 4)
             near = near_edge[:, i * LEAF_LEN : (i + 1) * LEAF_LEN]
-        out[:, l * LEAF_LEN : (l + 1) * LEAF_LEN] = near + total[:NRHS] + total[NRHS:]
+        staged[:, l * LEAF_LEN : (l + 1) * LEAF_LEN] = near + total[:NRHS] + total[NRHS:]
+        if l % PIECE == PIECE - 1:
+            part = pl.ds((l + 1 - PIECE) * LEAF_LEN, PIECE * LEAF_LEN)
+            copy = pltpu.make_async_copy(staged.at[:, part], out.at[:, part], sems.at[l // PIECE])
+            copy.start()
+            copies.append(copy)
+    for copy in copies:
+        copy.wait()
 
 
 VMEM = pl.BlockSpec(memory_space=pltpu.VMEM)
@@ -505,7 +514,11 @@
         final_kernel,
         out_shape=shape((NRHS, LEAVES * LEAF_LEN), F32),
         in_specs=[VMEM, SMEM, SMEM] + [VMEM] * 6,
-        out_specs=VMEM,
+        out_specs=HBM,
+        scratch_shapes=[
+            pltpu.VMEM((NRHS, LEAVES * LEAF_LEN), F32),
+            pltpu.SemaphoreType.DMA((LEAVES // PIECE,)),
+        ],
         compiler_params=LIMIT,
         cost_estimate=cost(2 * 10**7, 3 * 10**6),
     )(

time: 42.7 us -> 42.7 us (level)
  no operation moved by 1% of the time
where the time goes in v4:
time: 42.7 us; the launch traced here: 42.5 us
  starting transfers between devices  21.3 us (50%)
  Pallas kernels  17.3 us (41%)
  waiting for transfers between devices  3.7 us (9%)
    all_to_all x1, starting transfers between devices, body(): lax.all_to_all(blocks.reshape(NDEV, NRHS, 2 * RANK), AXES, 0, 0, axis_ind...  15.7 us
    pallas_call x1, Pallas kernels, body(): pl.pallas_call(inner_kernel, out_shape=(held((NRHS, (LEAVES - 4) * LEAF_L...  5.55 us
    pallas_call x1, Pallas kernels, body(): pl.pallas_call(edge_kernel, out_shape=(held((NRHS, 4 * LEAF_LEN), F32), h...  4.82 us
    ppermute x1, starting transfers between devices, body(): second = lax.ppermute(halo_second, AXES, seconds)  4.21 us
    pallas_call x1, Pallas kernels, body(): pl.pallas_call(up_kernel, out_shape=(shape(BOXES + (NRHS, 2 * RANK), BF16...  4.15 us
    all_to_all x1, waiting for transfers between devices, body(): lax.all_to_all(blocks.reshape(NDEV, NRHS, 2 * RANK), AXES, 0, 0, axis_ind...  3.69 us
    pallas_call x1, Pallas kernels, body(): pl.pallas_call(final_kernel, out_shape=shape((NRHS, LEAVES * LEAF_LEN), F...  2.77 us
    ppermute x1, starting transfers between devices, body(): first = lax.ppermute(halo_first, AXES, firsts)  1.47 us
  transfers between devices with their start and end apart: 3, of which 1 were waited for; matrix products, arithmetic and copies ran while one was open for 0% of the time, Pallas kernels for 24%

profile of v4, /device:TPU:1, one launch (start us, length us, event | category | flops | bytes accessed | tf_op | source)
XLA Modules:
  0.0 42.5 jit_solution(11385991176579829761)
XLA Ops:
  0.0 0.0 copy-start.3
  0.0 0.0 copy-start
  0.0 4.1 %shard_map.154 = (bf16[8,4,4,2,8,128]{5,4,3,2,1,0:T(8,128)(2,1)}, f32[28,8,64]{2,1,0:T(8,128)S(1)}, bf16[8,1152]{1,0:T(8,128)(2,1)S(1)}, bf16[8,1152]{1,0:T(8,12...) custom-call(bf16[8,4096]{1,0:T(8,128)(2,1)} %rhs_in.1, bf16[16,64,256]{2,1,0:T(8,128)(2,1)} %basis_in.2, ...), custom_call_target="tpu_custom_call" | custom-call | flops 20000000 | bytes 10000000 | tf_op jit(solution)/shard_map/pallas_call | solution.py:415
  4.2 15.7 %all-to-all-start = ((bf16[256,8,128]{2,1,0:T(8,128)(2,1)}), bf16[256,8,128]{2,1,0:T(8,128)(2,1)S(1)}, u32[]{:S(2)}, u32[]{:S(2)}) async-start(bf16[256,8,128]{2,1,0:T(8,128)(2,1)} %bitcast), calls=%async_computation | async-start | bytes 1048576 | tf_op jit(solution)/shard_map/all_to_all | solution.py:440
  19.8 1.5 %collective-permute-start = (bf16[8,1152]{1,0:T(8,128)(2,1)S(1)}, bf16[8,1152]{1,0:T(8,128)(2,1)S(1)}, u32[]{:S(2)}, u32[]{:S(2)}) collective-permute-start(bf16[8,1152]{1,0:T(8,128)(2,1)S(1)} %get-tuple-element.21), channel_id=1, source_target_pairs={{0,1},{1,0},{2,3},{3,2},{4,5},{5,4},{6,7},{7,6},{8,9},{9,8},{10,11... | collective-permute-start | bytes 55304 | tf_op jit(solution)/shard_map/ppermute | solution.py:447
  21.3 4.2 %collective-permute-start.1 = (bf16[8,1152]{1,0:T(8,128)(2,1)S(1)}, bf16[8,1152]{1,0:T(8,128)(2,1)S(1)}, u32[]{:S(2)}, u32[]{:S(2)}) collective-permute-start(bf16[8,1152]{1,0:T(8,128)(2,1)S(1)} %get-tuple-element.22), channel_id=1, source_target_pairs={{1,2},{2,1},{3,4},{4,3},{5,6},{6,5},{7,8},{8,7},{9,10},{10,9},{11,... | collective-permute-start | bytes 55304 | tf_op jit(solution)/shard_map/ppermute | solution.py:448
  25.5 0.0 copy-done.3
  25.5 0.0 copy-done
  25.5 0.0 copy-start.1
  25.6 0.0 copy-start.4
  25.6 5.6 %shard_map.155 = (f32[8,3072]{1,0:T(8,128)S(1)}, bf16[2,64,1024]{2,1,0:T(8,128)(2,1)S(1)}, f32[12,4,64,64]{3,2,1,0:T(8,128)S(1)}, f32[30,64,64]{2,1,0:T(8,128)S(1)}) custom-call(bf16[8,4096]{1,0:T(8,128)(2,1)S(1)} %get-tuple-element.20.rhs, bf16[6,3,256,256]{3,2,1,0:T(8,128)(2,1)S(1)} %get-tuple-element.24.near_early, bf16[16,3,256,256]{3,2,1,0:T(8,128)(2,1)} %near_in.5, ...), custom_call_target="tpu_custom_call" | custom-call | flops 200000000 | bytes 10000000 | tf_op jit(solution)/shard_map/pallas_call | solution.py:450
  31.1 0.0 collective-permute-done.first
  31.1 0.0 collective-permute-done.1.second
  31.2 0.0 copy-done.1
  31.2 0.0 copy-done.4
  31.2 0.0 copy-start.2
  31.2 0.0 copy-start.5
  31.2 4.8 %shard_map.156 = (f32[8,1024]{1,0:T(8,128)S(1)}, f32[8,1024]{1,0:T(8,128)S(1)}, bf16[2,2176,64]{2,1,0:T(8,128)(2,1)S(1)}, bf16[16,64,256]{2,1,0:T(8,128)(2,1)S(1)}) custom-call(bf16[8,4096]{1,0:T(8,128)(2,1)S(1)} %get-tuple-element.20.rhs, bf16[8,1152]{1,0:T(8,128)(2,1)S(1)} %collective-permute-done.first, ...), custom_call_target="tpu_custom_call" | custom-call | flops 100000000 | bytes 5000000 | tf_op jit(solution)/shard_map/pallas_call | solution.py:476
  36.0 3.7 %all-to-all-done = bf16[256,8,128]{2,1,0:T(8,128)(2,1)S(1)} async-done(((bf16[256,8,128]{2,1,0:T(8,128)(2,1)}), bf16[256,8,128]{2,1,0:T(8,128)(2,1)S(1)}, u32[]{:S(2)}, u32[]{:S(2)}) %all-to-all-start) | async-done | bytes 524320 | tf_op jit(solution)/shard_map/all_to_all | solution.py:440
  39.7 0.0 copy-done.2
  39.7 0.0 copy-done.5
  39.7 2.8 %shard_map.157 = f32[8,4096]{1,0:T(8,128)} custom-call(bf16[8,4,4,2,8,128]{5,4,3,2,1,0:T(8,128)(2,1)S(1)} %bitcast.5, s32[1,4,7]{2,1,0:T(4,128)S(1)} %bitcast.9, s32[1,7]{1,0:T(1,128)S(1)} %copy-done.5, bf16[2,2176,64]{2,1,0:T(8,128)(2,1)S(1)} %get-tuple-element.27.pairs, bf16[2,64,1024]{2,1,0:T(8,128)(2,1)S(1)} %get-tuple-element.28.paths, ...), custom_call_target="tpu_custom_call" | custom-call | flops 20000000 | bytes 3000000 | tf_op jit(solution)/shard_map/pallas_call | solution.py:513
Async XLA Ops:
  0.0 25.5 %copy-start.3 = (s32[16]{0:T(128)S(1)}, s32[16]{0:T(128)}, u32[]{:S(2)}) copy-start(s32[16]{0:T(128)} %count.4) | copy-start | bytes 196
  0.0 25.5 %copy-start = (s32[16,3]{0,1:T(4,128)S(1)}, s32[16,3]{0,1:T(4,128)}, u32[]{:S(2)}) copy-start(s32[16,3]{0,1:T(4,128)} %param.20) | copy-start | bytes 580
  4.2 35.6 %all-to-all-start = ((bf16[256,8,128]{2,1,0:T(8,128)(2,1)}), bf16[256,8,128]{2,1,0:T(8,128)(2,1)S(1)}, u32[]{:S(2)}, u32[]{:S(2)}) async-start(bf16[256,8,128]{2,1,0:T(8,128)(2,1)} %bitcast), calls=%async_computation | async-start | bytes 1048576 | tf_op jit(solution)/shard_map/all_to_all | solution.py:440
  19.8 11.3 %collective-permute-start = (bf16[8,1152]{1,0:T(8,128)(2,1)S(1)}, bf16[8,1152]{1,0:T(8,128)(2,1)S(1)}, u32[]{:S(2)}, u32[]{:S(2)}) collective-permute-start(bf16[8,1152]{1,0:T(8,128)(2,1)S(1)} %get-tuple-element.21), channel_id=1, source_target_pairs={{0,1},{1,0},{2,3},{3,2},{4,5},{5,4},{6,7},{7,6},{8,9},{9,8},{10,11... | collective-permute-start | bytes 55304 | tf_op jit(solution)/shard_map/ppermute | solution.py:447
  21.3 9.8 %collective-permute-start.1 = (bf16[8,1152]{1,0:T(8,128)(2,1)S(1)}, bf16[8,1152]{1,0:T(8,128)(2,1)S(1)}, u32[]{:S(2)}, u32[]{:S(2)}) collective-permute-start(bf16[8,1152]{1,0:T(8,128)(2,1)S(1)} %get-tuple-element.22), channel_id=1, source_target_pairs={{1,2},{2,1},{3,4},{4,3},{5,6},{6,5},{7,8},{8,7},{9,10},{10,9},{11,... | collective-permute-start | bytes 55304 | tf_op jit(solution)/shard_map/ppermute | solution.py:448
  25.5 5.6 %copy-start.1 = (s32[28,4]{0,1:T(4,128)S(1)}, s32[28,4]{0,1:T(4,128)}, u32[]{:S(2)}) copy-start(s32[28,4]{0,1:T(4,128)} %param.25) | copy-start | bytes 1348
  25.6 5.6 %copy-start.4 = (s32[28]{0:T(128)S(1)}, s32[28]{0:T(128)}, u32[]{:S(2)}) copy-start(s32[28]{0:T(128)} %local_count.1) | copy-start | bytes 340
  31.2 8.5 %copy-start.2 = (s32[1,7,4]{1,2,0:T(4,128)S(1)}, s32[1,7,4]{1,2,0:T(4,128)}, u32[]{:S(2)}) copy-start(s32[1,7,4]{1,2,0:T(4,128)} %param.30) | copy-start | bytes 340
  31.2 8.5 %copy-start.5 = (s32[1,7]{1,0:T(1,128)S(1)}, s32[1,7]{1,0:T(1,128)}, u32[]{:S(2)}) copy-start(s32[1,7]{1,0:T(1,128)} %count.5) | copy-start | bytes 88
